TPU v7x, 512 devices: a whole 4x4x16 slice. The times are simulated.
512 devices in a mesh: ctx: 32 (over y, z_hi, core), fsdp: 16 (over z_lo, x).
Axes of the slice: x: 4, y: 4, z: 16 (z_hi: 4, z_lo: 4; z = z_hi * 4 + z_lo), core: 2. Of those that a mesh axis runs over, the one named last changes fastest.
Arguments:
- events: bfloat16 [8192, 4096], P('ctx'), may hold values from -6 to 6
- tile_mask: int32 [64, 2], P('ctx'), may hold values 0 or 1
- initial_state: float32 [16, 128, 128], P('fsdp'), may hold values from -96 to 96
- w_query: bfloat16 [4096, 2048], P('ctx', 'fsdp'), may hold values from -0.09375 to 0.09375
- w_key: bfloat16 [4096, 2048], P('ctx', 'fsdp'), may hold values from -0.09375 to 0.09375
- w_value: bfloat16 [4096, 2048], P('ctx', 'fsdp'), may hold values from -0.09375 to 0.09375
- cotangent: bfloat16 [8192, 2048], P('ctx', 'fsdp'), may hold values from -6 to 6
Outputs:
- attended: bfloat16 [8192, 2048], P('ctx', 'fsdp')
- events_grad: bfloat16 [8192, 4096], P('ctx')
- query_grad: bfloat16 [4096, 2048], P('ctx', 'fsdp')
- key_grad: bfloat16 [4096, 2048], P('ctx', 'fsdp')
- value_grad: bfloat16 [4096, 2048], P('ctx', 'fsdp')
Inputs may be any that keep to these rules, and one draw needn't show every extreme that they name: `tile_mask`: only entries whose column is not above the row's tile place within its block of 256 events are read.
All inputs are finite; a program needn't handle non-finite values.
Results may differ from a plain program's by a relative error of at most 0.03.
Values may be sent and summed in bfloat16 or wider, within the bound.
No kernel may reach another device: no remote copies, remote signals or barrier semaphores. Data moves between devices by JAX's collectives and lax.ppermute only.
A program may use at most 64 MiB of HBM per device.

v0:
```python
import jax
import jax.numpy as jnp
from jax import lax
from jax.sharding import PartitionSpec as P

HDIM = 128
TILE = 128


epsilon = 1e-06


def prefix(array, axis, combine, identity, reverse):
    count, index = (lax.axis_size(axis), lax.axis_index(axis))
    everything = lax.all_gather(array.astype(jnp.bfloat16), axis)
    start = jnp.broadcast_to(jnp.asarray(identity, array.dtype), array.shape)

    def turn(k, before):
        at = count - 1 - k if reverse else k
        reached = at > index if reverse else at < index
        new = combine(before, everything[at].astype(array.dtype))
        return jnp.where(reached, new, before)

    return lax.fori_loop(0, count, turn, start)


def allowed_pairs(mask_block, tile):
    count = mask_block.shape[0]
    size = count * tile
    row_index = lax.broadcasted_iota(jnp.int32, (size, size), 0)
    col_index = lax.broadcasted_iota(jnp.int32, (size, size), 1)
    tiled = jnp.repeat(jnp.repeat(mask_block, tile, axis=0), tile, axis=1)
    return jnp.where((col_index <= row_index) & (tiled > 0), 1.0, 0.0).astype(jnp.float32)


def add_states(earlier, later):
    return earlier + later


def block_prefix(local_term, reverse):
    return prefix(local_term, "ctx", add_states, jnp.zeros_like(local_term), reverse)


def on_device(events, tile_mask, initial_state, w_query, w_key, w_value, cotangent):
    event_count, head_width = cotangent.shape
    head_count = head_width // HDIM
    stacked = jnp.stack((w_query, w_key, w_value))
    allowed = allowed_pairs(tile_mask, TILE)
    panels = lax.all_gather(stacked, "ctx", axis=1, tiled=True)
    projected = jnp.einsum("td,kdw->ktw", events, panels, preferred_element_type=jnp.float32)
    projected = projected.astype(jnp.bfloat16).reshape(3, event_count, head_count, HDIM)
    queries, key_rows, value_rows = (projected[0], projected[1], projected[2])
    local_state = jnp.einsum(
        "thd,the->hde", key_rows, value_rows, preferred_element_type=jnp.float32
    )
    carried_bf = (block_prefix(local_state, False) + initial_state).astype(jnp.bfloat16)
    scores = (
        jnp.einsum("thd,shd->hts", queries, key_rows, preferred_element_type=jnp.float32)
        * allowed[None]
    )
    mixing = scores.astype(jnp.bfloat16)
    mixture = jnp.einsum("hts,shd->thd", mixing, value_rows, preferred_element_type=jnp.float32)
    mixture = mixture + jnp.einsum(
        "thd,hde->the", queries, carried_bf, preferred_element_type=jnp.float32
    )
    inverse_rms = lax.rsqrt(jnp.mean(mixture * mixture, axis=-1, keepdims=True) + epsilon)
    attended = (mixture * inverse_rms).astype(jnp.bfloat16).reshape(event_count, head_width)
    upstream = cotangent.reshape(event_count, head_count, HDIM).astype(jnp.float32)
    mixture_grad = (
        inverse_rms * upstream
        - mixture * inverse_rms**3 * jnp.mean(upstream * mixture, axis=-1, keepdims=True)
    ).astype(jnp.bfloat16)
    score_grad = (
        jnp.einsum("the,she->hts", mixture_grad, value_rows, preferred_element_type=jnp.float32)
        * allowed[None]
    ).astype(jnp.bfloat16)
    local_grad = jnp.einsum(
        "thd,the->hde", queries, mixture_grad, preferred_element_type=jnp.float32
    )
    later_bf = block_prefix(local_grad, True).astype(jnp.bfloat16)
    query_part = jnp.einsum(
        "hts,shd->thd", score_grad, key_rows, preferred_element_type=jnp.float32
    )
    query_part = query_part + jnp.einsum(
        "the,hde->thd", mixture_grad, carried_bf, preferred_element_type=jnp.float32
    )
    key_part = jnp.einsum("hts,thd->shd", score_grad, queries, preferred_element_type=jnp.float32)
    key_part = key_part + jnp.einsum(
        "she,hde->shd", value_rows, later_bf, preferred_element_type=jnp.float32
    )
    value_part = jnp.einsum(
        "hts,the->she", mixing, mixture_grad, preferred_element_type=jnp.float32
    )
    value_part = value_part + jnp.einsum(
        "shd,hde->she", key_rows, later_bf, preferred_element_type=jnp.float32
    )
    grads = (
        jnp.stack((query_part, key_part, value_part))
        .astype(jnp.bfloat16)
        .reshape(3, event_count, head_width)
    )
    partial_grad = jnp.einsum("ktw,kdw->td", grads, panels, preferred_element_type=jnp.float32)
    events_grad = lax.psum(partial_grad.astype(jnp.bfloat16), "fsdp")
    summed = lax.psum_scatter(
        jnp.einsum("td,ktw->dkw", events, grads, preferred_element_type=jnp.float32).astype(
            jnp.bfloat16
        ),
        "ctx",
        scatter_dimension=0,
        tiled=True,
    )
    return (attended, events_grad, summed[:, 0], summed[:, 1], summed[:, 2])


def solution(mesh):
    placed = (
        P("ctx", None),
        P("ctx", None),
        P("fsdp", None, None),
        P("ctx", "fsdp"),
        P("ctx", "fsdp"),
        P("ctx", "fsdp"),
        P("ctx", "fsdp"),
    )
    return jax.shard_map(
        on_device,
        mesh=mesh,
        in_specs=placed,
        out_specs=(
            P("ctx", "fsdp"),
            P("ctx", None),
            P("ctx", "fsdp"),
            P("ctx", "fsdp"),
            P("ctx", "fsdp"),
        ),
        check_vma=False,
    )
```

profile of v0, /device:TPU:8, one launch (start us, length us, event | category | flops | bytes accessed | tf_op | source)
XLA Modules:
  0.0 613.5 jit_solution(2426722656759367331)
XLA Ops:
  7.2 1.0 copy.38
  8.2 0.9 copy.39
  9.1 0.9 copy.40
  10.8 97.0 %all-gather.6.cloned.1.call-done = bf16[3,4096,128]{1,2,0:T(8,128)(2,1)} async-done(((bf16[3,128,128]{1,2,0:T(8,128)(2,1)}), bf16[3,4096,128]{1,2,0:T(8,128)(2,1)}) %all-gather.6.cloned.1.call-update) | async-done | bytes 3145744 | tf_op jit(solution)/shard_map/all_gather | solution.py:49
  107.8 2.9 fusion.9
  112.3 63.8 %all-gather.8.cloned.1.call-done = bf16[4096,128]{1,0:T(8,128)(2,1)} async-done(((bf16[128,128]{1,0:T(8,128)(2,1)}), bf16[4096,128]{1,0:T(8,128)(2,1)}) %all-gather.8.cloned.1.call-update) | async-done | bytes 1048592 | tf_op jit(solution)/shard_map/all_gather | solution.py:15
  176.0 25.8 %while.30 = (s32[]{:T(128)}, f32[1,128,128]{2,1,0:T(8,128)S(1)}, s32[]{:T(128)}, bf16[32,1,128,128]{3,2,1,0:T(8,128)(2,1)}, s32[]{:T(128)}, /*index=5*/s32[]{:T(128)}) while((s32[]{:T(128)}, f32[1,128,128]{2,1,0:T(8,128)S(1)}, s32[]{:T(128)}, bf16[32,1,128,128]{3,2,1,0:T(8,128)(2,1)}, s32[]{:T(128)}, /*index=5*/s32[]{:T(128)}) %tuple.105), condition=%wide.region_1.2_spmd.clone, body=%wide.region_0.1_spmd.clone.sunk | while | flops 65540 | bytes 163941 | solution.py:24
  176.8 0.8 add_select_fusion.4
  177.7 0.8 add_select_fusion.4
  178.5 0.8 add_select_fusion.4
  180.9 0.8 add_select_fusion.4
  184.9 0.8 add_select_fusion.4
  188.1 0.8 add_select_fusion.4
  192.2 0.8 add_select_fusion.4
  196.2 0.8 add_select_fusion.4
  200.2 0.8 add_select_fusion.4
  203.8 65.0 %all-gather.10.cloned.1.call-done = bf16[4096,128]{1,0:T(8,128)(2,1)} async-done(((bf16[128,128]{1,0:T(8,128)(2,1)}), bf16[4096,128]{1,0:T(8,128)(2,1)}) %all-gather.10.cloned.1.call-update) | async-done | bytes 1048592 | tf_op jit(solution)/shard_map/all_gather | solution.py:15
  268.8 25.9 %while.31 = (s32[]{:T(128)}, f32[1,128,128]{2,1,0:T(8,128)S(1)}, s32[]{:T(128)}, bf16[32,1,128,128]{3,2,1,0:T(8,128)(2,1)}, s32[]{:T(128)}, /*index=5*/s32[]{:T(128)}, s32[]{:T(128)}, s32[]{:T(128)}) while((s32[]{:T(128)}, f32[1,128,128]{2,1,0:T(8,128)S(1)}, s32[]{:T(128)}, bf16[32,1,128,128]{3,2,1,0:T(8,128)(2,1)}, s32[]{:T(128)}, ...), condition=%wide.region_5.6_spmd.clone, body=%wide.region_4.5_spmd.clone.sunk | while | flops 65544 | bytes 164003 | solution.py:24
  269.6 0.8 add_select_fusion.5
  273.6 0.8 add_select_fusion.5
  276.1 0.8 add_select_fusion.5
  282.5 0.8 add_select_fusion.5
  285.0 0.8 add_select_fusion.5
  289.0 0.8 add_select_fusion.5
  291.5 0.8 add_select_fusion.5
  295.4 2.7 convolution_convert_fusion
  298.1 4.7 copy.56
  302.8 4.5 fusion
  308.1 118.9 %reduce-scatter.4.cloned.1.call-done = bf16[128,384]{1,0:T(8,128)(2,1)} async-done(((bf16[4096,384]{1,0:T(8,128)(2,1)}), bf16[128,384]{1,0:T(8,128)(2,1)}) %reduce-scatter.4.cloned.1.call-update) | async-done | bytes 98320
  427.0 1.0 copy.57
  430.2 173.7 %all-reduce.2.cloned.1.call-done = bf16[256,4096]{1,0:T(8,128)(2,1)} async-done(((bf16[256,4096]{1,0:T(8,128)(2,1)}), bf16[256,4096]{1,0:T(8,128)(2,1)}) %all-reduce.2.cloned.1.call-update) | async-done | bytes 2097168 | tf_op jit(solution)/shard_map/psum | solution.py:103
  603.8 3.1 copy.76
  (96 shorter events, 45.5 us)
Async XLA Ops:
  7.2 100.6 %copy-start = (bf16[256,4096]{1,0:T(8,128)(2,1)S(1)}, bf16[256,4096]{1,0:T(8,128)(2,1)}, u32[]{:S(2)}) copy-start(bf16[256,4096]{1,0:T(8,128)(2,1)} %param.11) | copy-start | bytes 6291460
  7.2 100.6 %all-gather.6.cloned.1.call-start = ((), (), s32[]{:S(2)}) async-start(), calls=%async_computation.1 | async-start | bytes 3244032 | tf_op jit(solution)/shard_map/all_gather | solution.py:49
  10.7 100.9 %copy-start.3 = (s32[2,2]{1,0:T(2,128)S(1)}, s32[2,2]{1,0:T(2,128)}, u32[]{:S(2)}) copy-start(s32[2,2]{1,0:T(2,128)} %param.12) | copy-start | bytes 52
  10.7 101.2 %copy-start.1 = (bf16[256,128]{1,0:T(8,128)(2,1)S(1)}, bf16[256,128]{1,0:T(8,128)(2,1)}, u32[]{:S(2)}) copy-start(bf16[256,128]{1,0:T(8,128)(2,1)} %param.17) | copy-start | bytes 196612
  10.7 191.1 %copy-start.2 = (f32[1,128,128]{2,1,0:T(8,128)S(1)}, f32[1,128,128]{2,1,0:T(8,128)}, u32[]{:S(2)}) copy-start(f32[1,128,128]{2,1,0:T(8,128)} %param.13) | copy-start | bytes 196612
  10.7 165.3 %all-gather.8.cloned.1.call-start = ((), (), s32[]{:S(2)}) async-start(), calls=%async_computation.3 | async-start | bytes 1081344 | tf_op jit(solution)/shard_map/all_gather | solution.py:15
  111.5 157.3 %all-gather.10.cloned.1.call-start = ((), (), s32[]{:S(2)}) async-start(), calls=%async_computation.4 | async-start | bytes 1081344 | tf_op jit(solution)/shard_map/all_gather | solution.py:15
  203.2 223.8 %reduce-scatter.4.cloned.1.call-start = ((), (), s32[]{:S(2)}) async-start(), calls=%async_computation.5 | async-start | bytes 3244032
  302.8 301.1 %all-reduce.2.cloned.1.call-start = ((), (), s32[]{:S(2)}) async-start(), calls=%async_computation.2 | async-start | bytes 4194304 | tf_op jit(solution)/shard_map/psum | solution.py:103
Sparse Core Ops, SparseCore 0:
  11.6 96.0 all-gather.5
  111.6 64.4 all-gather.7
  203.3 65.4 all-gather.9
  302.9 124.0 reduce-scatter.3
  430.6 173.1 all-reduce.1
where the time goes:
time: 618 us; the launch traced here: 613 us
  waiting for transfers between devices  518 us (84%)
  other arithmetic  50.9 us (8%)
  local copies, waits for them, and re-layouts  14.9 us (2%)
  between operations  14 us (2%)
  matrix products  13.5 us (2%)
    psum x1, waiting for transfers between devices, on_device(): events_grad = lax.psum(partial_grad.astype(jnp.bfloat16), 'fsdp')  174 us
    all_gather x2, waiting for transfers between devices, prefix(): everything = lax.all_gather(array.astype(jnp.bfloat16), axis)  129 us
    unnamed x6, waiting for transfers between devices  119 us
    all_gather x1, waiting for transfers between devices, on_device(): panels = lax.all_gather(stacked, 'ctx', axis=1, tiled=True)  97 us
    select_n x64, other arithmetic, turn(): return jnp.where(reached, new, before)  50.1 us
    unnamed x21, local copies, waits for them, and re-layouts  14.7 us
  transfers between devices with their start and end apart: 5, of which 5 were waited for; matrix products, arithmetic and copies ran while one was open for 2% of the time, Pallas kernels for 0%

commit v1 on v0

v1 whole, which is shorter than its diff:
```python
import jax
import jax.numpy as jnp
from jax import lax
from jax.sharding import Mesh
from jax.sharding import PartitionSpec as P

HDIM = 128
TILE = 128
CTX = ("y", "zh", "core")
FSDP = ("zl", "x")
SWAP = ((0, 1), (1, 0))
BF16, F32 = jnp.bfloat16, jnp.float32

epsilon = 1e-06


def dot(a, b, dims):
    return lax.dot_general(a, b, (dims, ((), ())), preferred_element_type=F32)


def mm(a, b):
    return dot(a, b, ((1,), (0,)))


def mt(a, b):
    return dot(a, b, ((1,), (1,)))


def tm(a, b):
    return dot(a, b, ((0,), (0,)))


def spread(array, axis):
    count = lax.axis_size(axis)
    return lax.all_to_all(jnp.broadcast_to(array[None], (count, *array.shape)), axis, 0, 0)


def trade(pieces, axis):
    return lax.all_to_all(pieces, axis, 0, 0)


def total(pieces):
    return jnp.sum(pieces.astype(F32), axis=0)


def swap(array):
    return lax.ppermute(array, "core", SWAP)


def allowed_pairs(mask_block):
    row_index = lax.broadcasted_iota(jnp.int32, (2 * TILE, 2 * TILE), 0)
    col_index = lax.broadcasted_iota(jnp.int32, (2 * TILE, 2 * TILE), 1)
    m = mask_block > 0
    lower = jnp.where(col_index < TILE, m[1, 0], m[1, 1])
    tiled = jnp.where(row_index < TILE, m[0, 0], lower)
    return (col_index <= row_index) & tiled


def scan_states(local, reverse, entering):
    blocks = 32
    rows = HDIM // blocks
    index = lax.axis_index(CTX)
    pieces = trade(local.astype(BF16).reshape(blocks, rows, HDIM), CTX)
    i = lax.broadcasted_iota(jnp.int32, (blocks, blocks), 0)
    j = lax.broadcasted_iota(jnp.int32, (blocks, blocks), 1)
    before = (j > i if reverse else j < i).astype(BF16)
    sums = mm(before, pieces.reshape(blocks, rows * HDIM)).reshape(blocks, rows, HDIM)
    if entering is not None:
        sums = sums + lax.dynamic_slice_in_dim(entering, index * rows, rows, 0)[None]
    return trade(sums.astype(BF16), CTX).reshape(HDIM, HDIM)


def gather_weights(shard):
    width = shard.shape[1]
    own = spread(spread(shard, "zh"), "y").reshape(2048, width)
    other = swap(own)
    back_own = trade(own.reshape(4, 512, width), "x")
    back_other = swap(back_own)
    return own, other, back_own, back_other


def scatter_grads(own, other):
    width = own.shape[1]
    mine = (own + swap(other.astype(BF16)).astype(F32)).astype(BF16)
    mine = total(trade(mine.reshape(4, 512, width), "y")).astype(BF16)
    return total(trade(mine.reshape(4, 128, width), "zh")).astype(BF16)


def on_device(events, tile_mask, initial_state, w_query, w_key, w_value, cotangent):
    first = lax.axis_index("core") == 0
    allowed = allowed_pairs(tile_mask)
    wkv, wkv_o, bkv, bkv_o = gather_weights(jnp.concatenate((w_key, w_value), axis=1))
    wq, wq_o, bq, bq_o = gather_weights(w_query)
    halves = events.reshape(256, 16, 2, 128)
    even, odd = halves[:, :, 0].reshape(256, 2048), halves[:, :, 1].reshape(256, 2048)
    ev, ev_o = jnp.where(first, even, odd), jnp.where(first, odd, even)

    kv = (mm(ev, wkv) + mm(ev_o, wkv_o)).astype(BF16)
    keys, values = kv[:, :128], kv[:, 128:]
    carried = scan_states(tm(keys, values), False, initial_state[0])
    queries = (mm(ev, wq) + mm(ev_o, wq_o)).astype(BF16)
    mixing = jnp.where(allowed, mt(queries, keys), 0.0).astype(BF16)
    mixture = mm(mixing, values) + mm(queries, carried)
    inverse_rms = lax.rsqrt(jnp.mean(mixture * mixture, axis=-1, keepdims=True) + epsilon)
    attended = (mixture * inverse_rms).astype(BF16)
    upstream = cotangent.astype(F32)
    mixture_grad = (
        inverse_rms * upstream
        - mixture * inverse_rms**3 * jnp.mean(upstream * mixture, axis=-1, keepdims=True)
    ).astype(BF16)
    later = scan_states(tm(queries, mixture_grad), True, None)
    score_grad = jnp.where(allowed, mt(mixture_grad, values), 0.0).astype(BF16)
    query_part = (mm(score_grad, keys) + mt(mixture_grad, carried)).astype(BF16)
    key_part = (tm(score_grad, queries) + mt(values, later)).astype(BF16)
    value_part = (tm(mixing, mixture_grad) + mm(keys, later)).astype(BF16)
    kv_part = jnp.concatenate((key_part, value_part), axis=1)

    def back(parts, own, other):
        seen = spread(parts, "x")
        a = sum(mt(seen[j], own[j]) for j in range(4))
        b = sum(mt(seen[j], other[j]) for j in range(4))
        return a, b

    qa, qb = back(query_part, bq, bq_o)
    ka, kb = back(kv_part, bkv, bkv_o)
    mine, others = (qa + ka).astype(BF16).reshape(256, 4, 1, 128), (qb + kb).astype(BF16).reshape(256, 4, 1, 128)
    term = jnp.where(
        first, jnp.concatenate((mine, others), 2), jnp.concatenate((others, mine), 2)
    ).reshape(256, 4, 256)
    summed = total(trade(term.transpose(1, 0, 2), "zl")).astype(BF16)
    whole = spread(spread(summed, "zl"), "x")
    events_grad = whole.transpose(2, 0, 1, 3).reshape(256, 4096)

    query_grad = scatter_grads(tm(ev, query_part), tm(ev_o, query_part))
    kv_grad = scatter_grads(tm(ev, kv_part), tm(ev_o, kv_part))
    return (attended, events_grad, query_grad, kv_grad[:, :128], kv_grad[:, 128:])


def solution(mesh):
    fine = Mesh(mesh.devices.reshape(4, 4, 2, 4, 4), CTX + FSDP)
    both = P(CTX, FSDP)
    return jax.shard_map(
        on_device,
        mesh=fine,
        in_specs=(P(CTX, None), P(CTX, None), P(FSDP, None, None), both, both, both, both),
        out_specs=(both, P(CTX, None), both, both, both),
        check_vma=False,
    )
```

time: 618 us -> 374 us (0.61)
  the two profiles are of different devices: /device:TPU:8 before, /device:TPU:1 now
where the time goes in v1:
time: 374 us; the launch traced here: 369 us
  waiting for transfers between devices  155 us (41%)
  starting transfers between devices  122 us (33%)
  matrix products  39.7 us (11%)
  local copies, waits for them, and re-layouts  21.8 us (6%)
  blocking collectives  19.4 us (5%)
  other arithmetic  9.84 us (3%)
    all_to_all x11, waiting for transfers between devices, trade(): return lax.all_to_all(pieces, axis, 0, 0)  92.5 us
    all_to_all x7, waiting for transfers between devices, spread(): lax.all_to_all(jnp.broadcast_to(array[None], (count, *array.shape)), axis...  60.1 us
    all_to_all x11, starting transfers between devices, trade(): return lax.all_to_all(pieces, axis, 0, 0)  48.9 us
    all_to_all x7, starting transfers between devices, spread(): lax.all_to_all(jnp.broadcast_to(array[None], (count, *array.shape)), axis...  44.8 us
    dot_general x38, matrix products, dot(): return lax.dot_general(a, b, (dims, ((), ())), preferred_element_type=F32)  39.7 us
    ppermute x6, starting transfers between devices, swap(): return lax.ppermute(array, 'core', SWAP)  28.7 us
    all_to_all x1, blocking collectives, spread(): lax.all_to_all(jnp.broadcast_to(array[None], (count, *array.shape)), axis...  19.4 us
    broadcast_in_dim x8, local copies, waits for them, and re-layouts, spread(): jnp.broadcast_to(array[None], (count, *array.shape))  7.71 us
  transfers between devices with their start and end apart: 24, of which 16 were waited for; matrix products, arithmetic and copies ran while one was open for 15% of the time, Pallas kernels for 0%

profile of v1, /device:TPU:1, one launch (start us, length us, event | category | flops | bytes accessed | tf_op | source)
XLA Modules:
  0.0 369.3 jit_solution(11368831541146247735)
XLA Ops:
  2.1 15.6 %all-to-all-start = ((bf16[4,128,128]{2,1,0:T(8,128)(2,1)}), bf16[4,128,128]{2,1,0:T(8,128)(2,1)S(1)}, u32[]{:S(2)}, u32[]{:S(2)}) async-start(bf16[4,128,128]{2,1,0:T(8,128)(2,1)} %broadcast_in_dim.36), calls=%async_computation | async-start | bytes 262144 | tf_op jit(solution)/shard_map/all_to_all | solution.py:35
  18.5 11.9 %all-to-all-done = bf16[4,128,128]{2,1,0:T(8,128)(2,1)S(1)} async-done(((bf16[4,128,128]{2,1,0:T(8,128)(2,1)}), bf16[4,128,128]{2,1,0:T(8,128)(2,1)S(1)}, u32[]{:S(2)}, u32[]{:S(2)}) %all-to-all-start) | async-done | bytes 131104 | tf_op jit(solution)/shard_map/all_to_all | solution.py:35
  30.4 19.4 %all_to_all.95 = bf16[4,128,256]{2,1,0:T(8,128)(2,1)S(1)} all-to-all(bf16[4,128,256]{2,1,0:T(8,128)(2,1)S(1)} %broadcast_in_dim.38), channel_id=1, replica_groups=mesh['y'=4,'zh'=4,'core'=2,'zl'=4,'x'=4] {'zh'}, dimensions={0} | all-to-all | bytes 524288 | tf_op jit(solution)/shard_map/all_to_all | solution.py:35
  51.0 4.2 %all-to-all-start.3 = ((bf16[4,4,128,256]{3,2,1,0:T(8,128)(2,1)}), bf16[4,4,128,256]{3,2,1,0:T(8,128)(2,1)}, u32[]{:S(2)}, u32[]{:S(2)}) async-start(bf16[4,4,128,256]{3,2,1,0:T(8,128)(2,1)} %broadcast_in_dim.39), calls=%async_computation.3 | async-start | bytes 2097152 | tf_op jit(solution)/shard_map/all_to_all | solution.py:35
  57.7 7.3 %all-to-all-done.3 = bf16[4,4,128,256]{3,2,1,0:T(8,128)(2,1)} async-done(((bf16[4,4,128,256]{3,2,1,0:T(8,128)(2,1)}), bf16[4,4,128,256]{3,2,1,0:T(8,128)(2,1)}, u32[]{:S(2)}, u32[]{:S(2)}) %all-to-all-start.3) | async-done | bytes 1048608 | tf_op jit(solution)/shard_map/all_to_all | solution.py:35
  65.9 4.1 %all-to-all-start.1 = ((bf16[4,4,128,128]{3,2,1,0:T(8,128)(2,1)}), bf16[4,4,128,128]{3,2,1,0:T(8,128)(2,1)}, u32[]{:S(2)}, u32[]{:S(2)}) async-start(bf16[4,4,128,128]{3,2,1,0:T(8,128)(2,1)} %broadcast_in_dim.37), calls=%async_computation.1 | async-start | bytes 1048576 | tf_op jit(solution)/shard_map/all_to_all | solution.py:35
  70.7 8.2 %collective-permute-start.1 = (bf16[2048,256]{1,0:T(8,128)(2,1)}, bf16[2048,256]{1,0:T(8,128)(2,1)}, u32[]{:S(2)}, u32[]{:S(2)}) collective-permute-start(bf16[2048,256]{1,0:T(8,128)(2,1)} %bitcast.7), channel_id=1, source_target_pairs={{0,16},{16,0},{1,17},{17,1},{2,18},{18,2},{3,19},{19,3},{4,20},{20... | collective-permute-start | bytes 3145736 | tf_op jit(solution)/shard_map/ppermute | solution.py:47
  80.6 4.0 %all-to-all-start.7 = ((bf16[4,512,128]{2,1,0:T(8,128)(2,1)}), bf16[4,512,128]{2,1,0:T(8,128)(2,1)S(1)}, u32[]{:S(2)}, u32[]{:S(2)}) async-start(bf16[4,512,128]{2,1,0:T(8,128)(2,1)} %bitcast.14), calls=%async_computation.7 | async-start | bytes 1048576 | tf_op jit(solution)/shard_map/all_to_all | solution.py:39
  86.1 6.1 %collective-permute-start = (bf16[2048,128]{1,0:T(8,128)(2,1)}, bf16[2048,128]{1,0:T(8,128)(2,1)}, u32[]{:S(2)}, u32[]{:S(2)}) collective-permute-start(bf16[2048,128]{1,0:T(8,128)(2,1)} %bitcast.5), channel_id=1, source_target_pairs={{0,16},{16,0},{1,17},{17,1},{2,18},{18,2},{3,19},{19,3},{4,20},{20... | collective-permute-start | bytes 1572872 | tf_op jit(solution)/shard_map/ppermute | solution.py:47
  93.7 5.1 %collective-permute-start.2 = (bf16[4,512,128]{2,1,0:T(8,128)(2,1)S(1)}, bf16[4,512,128]{2,1,0:T(8,128)(2,1)}, u32[]{:S(2)}, u32[]{:S(2)}) collective-permute-start(bf16[4,512,128]{2,1,0:T(8,128)(2,1)S(1)} %all-to-all-done.7), channel_id=1, source_target_pairs={{0,16},{16,0},{1,17},{17,1},{2,18},{18,2},{3,19},{19,3},{4,20},{20... | collective-permute-start | bytes 1572872 | tf_op jit(solution)/shard_map/ppermute | solution.py:47
  98.8 4.2 %all-to-all-start.11 = ((bf16[4,512,256]{2,1,0:T(8,128)(2,1)}), bf16[4,512,256]{2,1,0:T(8,128)(2,1)}, u32[]{:S(2)}, u32[]{:S(2)}) async-start(bf16[4,512,256]{2,1,0:T(8,128)(2,1)} %bitcast.27), calls=%async_computation.11 | async-start | bytes 2097152 | tf_op jit(solution)/shard_map/all_to_all | solution.py:39
  107.3 11.0 %all-to-all-done.11 = bf16[4,512,256]{2,1,0:T(8,128)(2,1)} async-done(((bf16[4,512,256]{2,1,0:T(8,128)(2,1)}), bf16[4,512,256]{2,1,0:T(8,128)(2,1)}, u32[]{:S(2)}, u32[]{:S(2)}) %all-to-all-start.11) | async-done | bytes 1048608 | tf_op jit(solution)/shard_map/all_to_all | solution.py:39
  118.3 7.9 %all-to-all-start.4 = ((bf16[32,4,128]{2,1,0:T(4,128)(2,1)}), bf16[32,4,128]{2,1,0:T(4,128)(2,1)S(1)}, u32[]{:S(2)}, u32[]{:S(2)}) async-start(bf16[32,4,128]{2,1,0:T(4,128)(2,1)} %bitcast.9), calls=%async_computation.4 | async-start | bytes 65536 | tf_op jit(solution)/shard_map/all_to_all | solution.py:39
  129.9 10.8 %all-to-all-done.4 = bf16[32,4,128]{2,1,0:T(4,128)(2,1)S(1)} async-done(((bf16[32,4,128]{2,1,0:T(4,128)(2,1)}), bf16[32,4,128]{2,1,0:T(4,128)(2,1)S(1)}, u32[]{:S(2)}, u32[]{:S(2)}) %all-to-all-start.4) | async-done | bytes 32800 | tf_op jit(solution)/shard_map/all_to_all | solution.py:39
  141.5 3.9 %all-to-all-start.5 = ((bf16[32,4,128]{2,1,0:T(4,128)(2,1)}), bf16[32,4,128]{2,1,0:T(4,128)(2,1)S(1)}, u32[]{:S(2)}, u32[]{:S(2)}) async-start(bf16[32,4,128]{2,1,0:T(4,128)(2,1)} %copy.70), calls=%async_computation.5 | async-start | bytes 65536 | tf_op jit(solution)/shard_map/all_to_all | solution.py:39
  146.3 13.8 %all-to-all-done.5 = bf16[32,4,128]{2,1,0:T(4,128)(2,1)S(1)} async-done(((bf16[32,4,128]{2,1,0:T(4,128)(2,1)}), bf16[32,4,128]{2,1,0:T(4,128)(2,1)S(1)}, u32[]{:S(2)}, u32[]{:S(2)}) %all-to-all-start.5) | async-done | bytes 32800 | tf_op jit(solution)/shard_map/all_to_all | solution.py:39
  170.6 10.9 %all-to-all-done.8 = bf16[32,4,128]{2,1,0:T(4,128)(2,1)S(1)} async-done(((bf16[32,4,128]{2,1,0:T(4,128)(2,1)}), bf16[32,4,128]{2,1,0:T(4,128)(2,1)S(1)}, u32[]{:S(2)}, u32[]{:S(2)}) %all-to-all-start.8) | async-done | bytes 32800 | tf_op jit(solution)/shard_map/all_to_all | solution.py:39
  186.4 5.3 %all-to-all-done.6 = bf16[4,256,128]{2,1,0:T(8,128)(2,1)S(1)} async-done(((bf16[4,256,128]{2,1,0:T(8,128)(2,1)}), bf16[4,256,128]{2,1,0:T(8,128)(2,1)S(1)}, u32[]{:S(2)}, u32[]{:S(2)}) %all-to-all-start.6) | async-done | bytes 262176 | tf_op jit(solution)/shard_map/all_to_all | solution.py:35
  191.7 5.0 %all-to-all-start.9 = ((bf16[32,4,128]{2,1,0:T(4,128)(2,1)}), bf16[32,4,128]{2,1,0:T(4,128)(2,1)S(1)}, u32[]{:S(2)}, u32[]{:S(2)}) async-start(bf16[32,4,128]{2,1,0:T(4,128)(2,1)} %copy.73), calls=%async_computation.9 | async-start | bytes 65536 | tf_op jit(solution)/shard_map/all_to_all | solution.py:39
  202.4 9.0 %all-to-all-done.9 = bf16[32,4,128]{2,1,0:T(4,128)(2,1)S(1)} async-done(((bf16[32,4,128]{2,1,0:T(4,128)(2,1)}), bf16[32,4,128]{2,1,0:T(4,128)(2,1)S(1)}, u32[]{:S(2)}, u32[]{:S(2)}) %all-to-all-start.9) | async-done | bytes 32800 | tf_op jit(solution)/shard_map/all_to_all | solution.py:39
  221.7 4.9 %all-to-all-done.10 = bf16[4,256,256]{2,1,0:T(8,128)(2,1)S(1)} async-done(((bf16[4,256,256]{2,1,0:T(8,128)(2,1)}), bf16[4,256,256]{2,1,0:T(8,128)(2,1)S(1)}, u32[]{:S(2)}, u32[]{:S(2)}) %all-to-all-start.10) | async-done | bytes 524320 | tf_op jit(solution)/shard_map/all_to_all | solution.py:35
  226.6 4.1 %all-to-all-start.15 = ((bf16[4,512,128]{2,1,0:T(8,128)(2,1)}), bf16[4,512,128]{2,1,0:T(8,128)(2,1)}, u32[]{:S(2)}, u32[]{:S(2)}) async-start(bf16[4,512,128]{2,1,0:T(8,128)(2,1)} %bitcast.47), calls=%async_computation.15 | async-start | bytes 1048576 | tf_op jit(solution)/shard_map/all_to_all | solution.py:39
  253.2 9.2 %all-to-all-done.16 = bf16[4,128,128]{2,1,0:T(8,128)(2,1)S(1)} async-done(((bf16[4,128,128]{2,1,0:T(8,128)(2,1)}), bf16[4,128,128]{2,1,0:T(8,128)(2,1)S(1)}, u32[]{:S(2)}, u32[]{:S(2)}) %all-to-all-start.16) | async-done | bytes 131104 | tf_op jit(solution)/shard_map/all_to_all | solution.py:39
  262.4 4.9 %all-to-all-start.12 = ((bf16[4,256,256]{1,2,0:T(8,128)(2,1)}), bf16[4,256,256]{1,2,0:T(8,128)(2,1)S(1)}, u32[]{:S(2)}, u32[]{:S(2)}) async-start(bf16[4,256,256]{1,2,0:T(8,128)(2,1)} %bitcast.44), calls=%async_computation.12 | async-start | bytes 1048576 | tf_op jit(solution)/shard_map/all_to_all | solution.py:39
  267.8 5.0 %collective-permute-start.5 = (bf16[2048,256]{1,0:T(8,128)(2,1)S(1)}, bf16[2048,256]{1,0:T(8,128)(2,1)S(1)}, u32[]{:S(2)}, u32[]{:S(2)}) collective-permute-start(bf16[2048,256]{1,0:T(8,128)(2,1)S(1)} %convolution_convert_fusion), channel_id=1, source_target_pairs={{0,16},{16,0},{1,17},{17,1},{2,18},{18,2},{3,19},{19,3},{4,20},{20... | collective-permute-start | bytes 3145736 | tf_op jit(solution)/shard_map/ppermute | solution.py:47
  282.4 9.6 %all-to-all-done.17 = bf16[4,512,256]{2,1,0:T(8,128)(2,1)S(1)} async-done(((bf16[4,512,256]{2,1,0:T(8,128)(2,1)}), bf16[4,512,256]{2,1,0:T(8,128)(2,1)S(1)}, u32[]{:S(2)}, u32[]{:S(2)}) %all-to-all-start.17) | async-done | bytes 1048608 | tf_op jit(solution)/shard_map/all_to_all | solution.py:39
  292.8 10.2 %all-to-all-start.13 = ((bf16[4,256,256]{2,1,0:T(8,128)(2,1)}), bf16[4,256,256]{2,1,0:T(8,128)(2,1)S(1)}, u32[]{:S(2)}, u32[]{:S(2)}) async-start(bf16[4,256,256]{2,1,0:T(8,128)(2,1)} %broadcast_in_dim.78), calls=%async_computation.13 | async-start | bytes 1048576 | tf_op jit(solution)/shard_map/all_to_all | solution.py:35
  303.9 10.7 %all-to-all-done.13 = bf16[4,256,256]{2,1,0:T(8,128)(2,1)S(1)} async-done(((bf16[4,256,256]{2,1,0:T(8,128)(2,1)}), bf16[4,256,256]{2,1,0:T(8,128)(2,1)S(1)}, u32[]{:S(2)}, u32[]{:S(2)}) %all-to-all-start.13) | async-done | bytes 524320 | tf_op jit(solution)/shard_map/all_to_all | solution.py:35
  314.6 3.9 %all-to-all-start.18 = ((bf16[4,128,256]{2,1,0:T(8,128)(2,1)}), bf16[4,128,256]{2,1,0:T(8,128)(2,1)S(1)}, u32[]{:S(2)}, u32[]{:S(2)}) async-start(bf16[4,128,256]{2,1,0:T(8,128)(2,1)} %bitcast.50), calls=%async_computation.18 | async-start | bytes 524288 | tf_op jit(solution)/shard_map/all_to_all | solution.py:39
  318.9 16.1 %all-to-all-done.18 = bf16[4,128,256]{2,1,0:T(8,128)(2,1)S(1)} async-done(((bf16[4,128,256]{2,1,0:T(8,128)(2,1)}), bf16[4,128,256]{2,1,0:T(8,128)(2,1)S(1)}, u32[]{:S(2)}, u32[]{:S(2)}) %all-to-all-start.18) | async-done | bytes 262176 | tf_op jit(solution)/shard_map/all_to_all | solution.py:39
  342.7 20.0 %all-to-all-done.14 = bf16[4,4,256,256]{3,1,2,0:T(4,128)(2,1)S(1)} async-done(((bf16[4,4,256,256]{3,1,2,0:T(4,128)(2,1)}), bf16[4,4,256,256]{3,1,2,0:T(4,128)(2,1)S(1)}, u32[]{:S(2)}, u32[]{:S(2)}) %all-to-all-start.14) | async-done | bytes 2097184 | tf_op jit(solution)/shard_map/all_to_all | solution.py:35
  365.2 4.1 %copy.83 = bf16[256,4096]{1,0:T(8,128)(2,1)} copy(bf16[256,4096]{0,1:T(8,128)(2,1)} %bitcast.179) | data formatting | bytes 4194304
  (110 shorter events, 97.4 us)
Async XLA Ops:
  0.6 85.4 %copy-start = (f32[1,128,128]{2,1,0:T(8,128)S(1)}, f32[1,128,128]{2,1,0:T(8,128)}, u32[]{:S(2)}) copy-start(f32[1,128,128]{2,1,0:T(8,128)} %param.9) | copy-start | bytes 196612
  2.1 28.3 %all-to-all-start = ((bf16[4,128,128]{2,1,0:T(8,128)(2,1)}), bf16[4,128,128]{2,1,0:T(8,128)(2,1)S(1)}, u32[]{:S(2)}, u32[]{:S(2)}) async-start(bf16[4,128,128]{2,1,0:T(8,128)(2,1)} %broadcast_in_dim.36), calls=%async_computation | async-start | bytes 262144 | tf_op jit(solution)/shard_map/all_to_all | solution.py:35
  18.5 36.7 %copy-start.1 = (bf16[256,4096]{1,0:T(8,128)(2,1)S(1)}, bf16[256,4096]{1,0:T(8,128)(2,1)}, u32[]{:S(2)}) copy-start(bf16[256,4096]{1,0:T(8,128)(2,1)} %param.7) | copy-start | bytes 6291460
  51.0 14.1 %all-to-all-start.3 = ((bf16[4,4,128,256]{3,2,1,0:T(8,128)(2,1)}), bf16[4,4,128,256]{3,2,1,0:T(8,128)(2,1)}, u32[]{:S(2)}, u32[]{:S(2)}) async-start(bf16[4,4,128,256]{3,2,1,0:T(8,128)(2,1)} %broadcast_in_dim.39), calls=%async_computation.3 | async-start | bytes 2097152 | tf_op jit(solution)/shard_map/all_to_all | solution.py:35
  65.9 14.6 %all-to-all-start.1 = ((bf16[4,4,128,128]{3,2,1,0:T(8,128)(2,1)}), bf16[4,4,128,128]{3,2,1,0:T(8,128)(2,1)}, u32[]{:S(2)}, u32[]{:S(2)}) async-start(bf16[4,4,128,128]{3,2,1,0:T(8,128)(2,1)} %broadcast_in_dim.37), calls=%async_computation.1 | async-start | bytes 1048576 | tf_op jit(solution)/shard_map/all_to_all | solution.py:35
  70.7 34.1 %collective-permute-start.1 = (bf16[2048,256]{1,0:T(8,128)(2,1)}, bf16[2048,256]{1,0:T(8,128)(2,1)}, u32[]{:S(2)}, u32[]{:S(2)}) collective-permute-start(bf16[2048,256]{1,0:T(8,128)(2,1)} %bitcast.7), channel_id=1, source_target_pairs={{0,16},{16,0},{1,17},{17,1},{2,18},{18,2},{3,19},{19,3},{4,20},{20... | collective-permute-start | bytes 3145736 | tf_op jit(solution)/shard_map/ppermute | solution.py:47
  78.8 7.1 %copy-start.7 = (bf16[256,128]{1,0:T(8,128)(2,1)S(1)}, bf16[256,128]{1,0:T(8,128)(2,1)}, u32[]{:S(2)}) copy-start(bf16[256,128]{1,0:T(8,128)(2,1)} %param.13) | copy-start | bytes 196612
  80.6 13.1 %all-to-all-start.7 = ((bf16[4,512,128]{2,1,0:T(8,128)(2,1)}), bf16[4,512,128]{2,1,0:T(8,128)(2,1)S(1)}, u32[]{:S(2)}, u32[]{:S(2)}) async-start(bf16[4,512,128]{2,1,0:T(8,128)(2,1)} %bitcast.14), calls=%async_computation.7 | async-start | bytes 1048576 | tf_op jit(solution)/shard_map/all_to_all | solution.py:39
  86.1 40.2 %collective-permute-start = (bf16[2048,128]{1,0:T(8,128)(2,1)}, bf16[2048,128]{1,0:T(8,128)(2,1)}, u32[]{:S(2)}, u32[]{:S(2)}) collective-permute-start(bf16[2048,128]{1,0:T(8,128)(2,1)} %bitcast.5), channel_id=1, source_target_pairs={{0,16},{16,0},{1,17},{17,1},{2,18},{18,2},{3,19},{19,3},{4,20},{20... | collective-permute-start | bytes 1572872 | tf_op jit(solution)/shard_map/ppermute | solution.py:47
  93.7 104.8 %collective-permute-start.2 = (bf16[4,512,128]{2,1,0:T(8,128)(2,1)S(1)}, bf16[4,512,128]{2,1,0:T(8,128)(2,1)}, u32[]{:S(2)}, u32[]{:S(2)}) collective-permute-start(bf16[4,512,128]{2,1,0:T(8,128)(2,1)S(1)} %all-to-all-done.7), channel_id=1, source_target_pairs={{0,16},{16,0},{1,17},{17,1},{2,18},{18,2},{3,19},{19,3},{4,20},{20... | collective-permute-start | bytes 1572872 | tf_op jit(solution)/shard_map/ppermute | solution.py:47
  98.8 19.6 %all-to-all-start.11 = ((bf16[4,512,256]{2,1,0:T(8,128)(2,1)}), bf16[4,512,256]{2,1,0:T(8,128)(2,1)}, u32[]{:S(2)}, u32[]{:S(2)}) async-start(bf16[4,512,256]{2,1,0:T(8,128)(2,1)} %bitcast.27), calls=%async_computation.11 | async-start | bytes 2097152 | tf_op jit(solution)/shard_map/all_to_all | solution.py:39
  118.3 22.4 %all-to-all-start.4 = ((bf16[32,4,128]{2,1,0:T(4,128)(2,1)}), bf16[32,4,128]{2,1,0:T(4,128)(2,1)S(1)}, u32[]{:S(2)}, u32[]{:S(2)}) async-start(bf16[32,4,128]{2,1,0:T(4,128)(2,1)} %bitcast.9), calls=%async_computation.4 | async-start | bytes 65536 | tf_op jit(solution)/shard_map/all_to_all | solution.py:39
  127.8 104.2 %collective-permute-start.3 = (bf16[4,512,256]{2,1,0:T(8,128)(2,1)}, bf16[4,512,256]{2,1,0:T(8,128)(2,1)}, u32[]{:S(2)}, u32[]{:S(2)}) collective-permute-start(bf16[4,512,256]{2,1,0:T(8,128)(2,1)} %all-to-all-done.11), channel_id=1, source_target_pairs={{0,16},{16,0},{1,17},{17,1},{2,18},{18,2},{3,19},{19,3},{4,20},{20... | collective-permute-start | bytes 3145736 | tf_op jit(solution)/shard_map/ppermute | solution.py:47
  141.5 18.6 %all-to-all-start.5 = ((bf16[32,4,128]{2,1,0:T(4,128)(2,1)}), bf16[32,4,128]{2,1,0:T(4,128)(2,1)S(1)}, u32[]{:S(2)}, u32[]{:S(2)}) async-start(bf16[32,4,128]{2,1,0:T(4,128)(2,1)} %copy.70), calls=%async_computation.5 | async-start | bytes 65536 | tf_op jit(solution)/shard_map/all_to_all | solution.py:39
  146.3 15.8 %copy-start.5 = (bf16[256,256]{1,0:T(8,128)(2,1)}, bf16[256,256]{1,0:T(8,128)(2,1)S(1)}, u32[]{:S(2)}) copy-start(bf16[256,256]{1,0:T(8,128)(2,1)S(1)} %fusion.9) | copy-start | bytes 393220
  163.1 18.4 %all-to-all-start.8 = ((bf16[32,4,128]{2,1,0:T(4,128)(2,1)}), bf16[32,4,128]{2,1,0:T(4,128)(2,1)S(1)}, u32[]{:S(2)}, u32[]{:S(2)}) async-start(bf16[32,4,128]{2,1,0:T(4,128)(2,1)} %bitcast.23), calls=%async_computation.8 | async-start | bytes 65536 | tf_op jit(solution)/shard_map/all_to_all | solution.py:39
  168.4 51.0 %collective-permute-start.4 = (bf16[2048,128]{1,0:T(8,128)(2,1)}, bf16[2048,128]{1,0:T(8,128)(2,1)}, u32[]{:S(2)}, u32[]{:S(2)}) collective-permute-start(bf16[2048,128]{1,0:T(8,128)(2,1)} %convolution_convert_fusion.1), channel_id=1, source_target_pairs={{0,16},{16,0},{1,17},{17,1},{2,18},{18,2},{3,19},{19,3},{4,20},{20... | collective-permute-start | bytes 1572872 | tf_op jit(solution)/shard_map/ppermute | solution.py:47
  182.3 9.5 %all-to-all-start.6 = ((bf16[4,256,128]{2,1,0:T(8,128)(2,1)}), bf16[4,256,128]{2,1,0:T(8,128)(2,1)S(1)}, u32[]{:S(2)}, u32[]{:S(2)}) async-start(bf16[4,256,128]{2,1,0:T(8,128)(2,1)} %broadcast_in_dim.41), calls=%async_computation.6 | async-start | bytes 524288 | tf_op jit(solution)/shard_map/all_to_all | solution.py:35
  191.7 19.6 %all-to-all-start.9 = ((bf16[32,4,128]{2,1,0:T(4,128)(2,1)}), bf16[32,4,128]{2,1,0:T(4,128)(2,1)S(1)}, u32[]{:S(2)}, u32[]{:S(2)}) async-start(bf16[32,4,128]{2,1,0:T(4,128)(2,1)} %copy.73), calls=%async_computation.9 | async-start | bytes 65536 | tf_op jit(solution)/shard_map/all_to_all | solution.py:39
  213.0 8.7 %copy-start.3 = (bf16[256,128]{0,1:T(8,128)(2,1)}, bf16[256,128]{0,1:T(8,128)(2,1)S(1)}, u32[]{:S(2)}) copy-start(bf16[256,128]{0,1:T(8,128)(2,1)S(1)} %fusion.14) | copy-start | bytes 196612
  214.0 12.6 %all-to-all-start.10 = ((bf16[4,256,256]{2,1,0:T(8,128)(2,1)}), bf16[4,256,256]{2,1,0:T(8,128)(2,1)S(1)}, u32[]{:S(2)}, u32[]{:S(2)}) async-start(bf16[4,256,256]{2,1,0:T(8,128)(2,1)} %broadcast_in_dim.42), calls=%async_computation.10 | async-start | bytes 1048576 | tf_op jit(solution)/shard_map/all_to_all | solution.py:35
  226.6 17.7 %all-to-all-start.15 = ((bf16[4,512,128]{2,1,0:T(8,128)(2,1)}), bf16[4,512,128]{2,1,0:T(8,128)(2,1)}, u32[]{:S(2)}, u32[]{:S(2)}) async-start(bf16[4,512,128]{2,1,0:T(8,128)(2,1)} %bitcast.47), calls=%async_computation.15 | async-start | bytes 1048576 | tf_op jit(solution)/shard_map/all_to_all | solution.py:39
  234.0 4.5 %copy-start.2 = (f32[256,512]{1,0:T(8,128)S(1)}, f32[256,512]{1,0:T(8,128)}, u32[]{:S(2)}) copy-start(f32[256,512]{1,0:T(8,128)} %convolution_add_fusion.1) | copy-start | bytes 1572868
  246.1 16.2 %all-to-all-start.16 = ((bf16[4,128,128]{2,1,0:T(8,128)(2,1)}), bf16[4,128,128]{2,1,0:T(8,128)(2,1)S(1)}, u32[]{:S(2)}, u32[]{:S(2)}) async-start(bf16[4,128,128]{2,1,0:T(8,128)(2,1)} %bitcast.48), calls=%async_computation.16 | async-start | bytes 262144 | tf_op jit(solution)/shard_map/all_to_all | solution.py:39
  249.4 17.9 %copy-start.4 = (bf16[256,128]{0,1:T(8,128)(2,1)S(1)}, bf16[256,128]{0,1:T(8,128)(2,1)}, u32[]{:S(2)}) copy-start(bf16[256,128]{0,1:T(8,128)(2,1)} %copy-done.3) | copy-start | bytes 196612
  262.4 16.1 %all-to-all-start.12 = ((bf16[4,256,256]{1,2,0:T(8,128)(2,1)}), bf16[4,256,256]{1,2,0:T(8,128)(2,1)S(1)}, u32[]{:S(2)}, u32[]{:S(2)}) async-start(bf16[4,256,256]{1,2,0:T(8,128)(2,1)} %bitcast.44), calls=%async_computation.12 | async-start | bytes 1048576 | tf_op jit(solution)/shard_map/all_to_all | solution.py:39
  267.8 7.2 %collective-permute-start.5 = (bf16[2048,256]{1,0:T(8,128)(2,1)S(1)}, bf16[2048,256]{1,0:T(8,128)(2,1)S(1)}, u32[]{:S(2)}, u32[]{:S(2)}) collective-permute-start(bf16[2048,256]{1,0:T(8,128)(2,1)S(1)} %convolution_convert_fusion), channel_id=1, source_target_pairs={{0,16},{16,0},{1,17},{17,1},{2,18},{18,2},{3,19},{19,3},{4,20},{20... | collective-permute-start | bytes 3145736 | tf_op jit(solution)/shard_map/ppermute | solution.py:47
  278.5 13.5 %all-to-all-start.17 = ((bf16[4,512,256]{2,1,0:T(8,128)(2,1)}), bf16[4,512,256]{2,1,0:T(8,128)(2,1)S(1)}, u32[]{:S(2)}, u32[]{:S(2)}) async-start(bf16[4,512,256]{2,1,0:T(8,128)(2,1)} %bitcast.49), calls=%async_computation.17 | async-start | bytes 2097152 | tf_op jit(solution)/shard_map/all_to_all | solution.py:39
  292.8 21.8 %all-to-all-start.13 = ((bf16[4,256,256]{2,1,0:T(8,128)(2,1)}), bf16[4,256,256]{2,1,0:T(8,128)(2,1)S(1)}, u32[]{:S(2)}, u32[]{:S(2)}) async-start(bf16[4,256,256]{2,1,0:T(8,128)(2,1)} %broadcast_in_dim.78), calls=%async_computation.13 | async-start | bytes 1048576 | tf_op jit(solution)/shard_map/all_to_all | solution.py:35
  314.6 20.4 %all-to-all-start.18 = ((bf16[4,128,256]{2,1,0:T(8,128)(2,1)}), bf16[4,128,256]{2,1,0:T(8,128)(2,1)S(1)}, u32[]{:S(2)}, u32[]{:S(2)}) async-start(bf16[4,128,256]{2,1,0:T(8,128)(2,1)} %bitcast.50), calls=%async_computation.18 | async-start | bytes 524288 | tf_op jit(solution)/shard_map/all_to_all | solution.py:39
  336.9 3.8 %copy-start.6 = (bf16[256,128]{0,1:T(8,128)(2,1)S(1)}, bf16[256,128]{0,1:T(8,128)(2,1)}, u32[]{:S(2)}) copy-start(bf16[256,128]{0,1:T(8,128)(2,1)} %get-tuple-element.40) | copy-start | bytes 196612
  336.9 25.8 %all-to-all-start.14 = ((bf16[4,4,256,256]{3,1,2,0:T(4,128)(2,1)}), bf16[4,4,256,256]{3,1,2,0:T(4,128)(2,1)S(1)}, u32[]{:S(2)}, u32[]{:S(2)}) async-start(bf16[4,4,256,256]{3,1,2,0:T(4,128)(2,1)} %broadcast_in_dim.79), calls=%async_computation.14 | async-start | bytes 4194304 | tf_op jit(solution)/shard_map/all_to_all | solution.py:35
  (1 other events, 2.5 us)

commit v2 on v1

v2 whole, which is shorter than its diff:
```python
import jax
import jax.numpy as jnp
from jax import lax
from jax.experimental import pallas as pl
from jax.experimental.pallas import tpu as pltpu
from jax.sharding import Mesh
from jax.sharding import PartitionSpec as P

HDIM = 128
TILE = 128
CTX = ("y", "zh", "core")
FSDP = ("zl", "x")
SWAP = ((0, 1), (1, 0))
BF16, F32 = jnp.bfloat16, jnp.float32

epsilon = 1e-06


def dot(a, b, dims):
    return lax.dot_general(a, b, (dims, ((), ())), preferred_element_type=F32)


def mm(a, b):
    return dot(a, b, ((1,), (0,)))


def mt(a, b):
    return dot(a, b, ((1,), (1,)))


def tm(a, b):
    return dot(a, b, ((0,), (0,)))


def spread(array, axis):
    count = lax.axis_size(axis)
    return lax.all_to_all(jnp.broadcast_to(array[None], (count, *array.shape)), axis, 0, 0)


def trade(pieces, axis):
    return lax.all_to_all(pieces, axis, 0, 0)


def total(pieces):
    return jnp.sum(pieces.astype(F32), axis=0)


def swap(array):
    return lax.ppermute(array, "core", SWAP)


def allowed_pairs(mask_block):
    row_index = lax.broadcasted_iota(jnp.int32, (2 * TILE, 2 * TILE), 0)
    col_index = lax.broadcasted_iota(jnp.int32, (2 * TILE, 2 * TILE), 1)
    m = mask_block > 0
    lower = jnp.where(col_index < TILE, m[1, 0], m[1, 1])
    tiled = jnp.where(row_index < TILE, m[0, 0], lower)
    return (col_index <= row_index) & tiled


def scan_states(local, reverse, entering):
    chip, y = lax.axis_index(("zh", "core")), lax.axis_index("y")

    def reached(pieces, at):
        index = lax.broadcasted_iota(jnp.int32, (pieces.shape[0], 1, 1), 0)
        return jnp.sum(jnp.where(index > at if reverse else index < at, pieces, 0.0), axis=0)

    near = lax.all_gather(local.astype(BF16), ("zh", "core")).astype(F32)
    before = reached(near, chip)
    if entering is not None:
        before = before + entering
    lines = spread(jnp.sum(near, axis=0).astype(BF16), "y").astype(F32)
    return (before + reached(lines, y)).astype(BF16)


def params(steps_bytes, flops):
    return dict(
        compiler_params=pltpu.CompilerParams(vmem_limit_bytes=40 * 2**20),
        cost_estimate=pl.CostEstimate(flops=flops, bytes_accessed=steps_bytes, transcendentals=0),
    )


def half(core, which):
    return pl.ds(pl.multiple_of((core if which == 0 else 1 - core) * 128, 128), 128)


def project_kernel(ids, events, own, other, out, acc, both):
    step, core = pl.program_id(0), ids[0]

    @pl.when(step == 0)
    def _():
        acc[...] = jnp.zeros_like(acc)

    total = acc[...]
    for i in range(4):
        both[half(core, 0), :] = own[i]
        both[half(core, 1), :] = other[i]
        total = total + mm(events[:, i * 256 : (i + 1) * 256], both[...])
    acc[...] = total

    @pl.when(step == 3)
    def _():
        out[...] = acc[...].astype(BF16)


def project(ids, events, own, other):
    width = own.shape[-1]
    weights = pl.BlockSpec((4, 128, width), lambda g, _: (g, 0, 0))
    return pl.pallas_call(
        project_kernel,
        out_shape=jax.ShapeDtypeStruct((256, width), BF16),
        grid_spec=pltpu.PrefetchScalarGridSpec(
            num_scalar_prefetch=1,
            grid=(4,),
            in_specs=[pl.BlockSpec((256, 1024), lambda g, _: (0, g)), weights, weights],
            out_specs=pl.BlockSpec((256, width), lambda g, _: (0, 0)),
            scratch_shapes=[pltpu.VMEM((256, width), F32), pltpu.VMEM((256, width), BF16)],
        ),
        **params(5 * 2**20, 2 * 256 * 4096 * width),
    )(ids, events, own, other)


def pick_kernel(ids, own, after, *pieces):
    for k in range(4):
        pieces[k][...] = own[lax.rem(ids[1] + k, 4)]


def pick(ids, own, after):
    _, rows, width = own.shape
    whole = pl.BlockSpec(memory_space=pltpu.VMEM)
    return pl.pallas_call(
        pick_kernel,
        out_shape=[jax.ShapeDtypeStruct((rows, width), BF16)] * 4,
        in_specs=[pl.BlockSpec(memory_space=pltpu.SMEM), whole, pl.BlockSpec(memory_space=pl.ANY)],
        out_specs=[whole] * 4,
        **params(3 * 2**20, 0),
    )(ids, own, after)


def grads_kernel(ids, events, parts, after, own, other):
    for i in range(4):
        term = tm(events[:, i * 256 : (i + 1) * 256], parts[...]).astype(BF16)

        @pl.when(ids[0] == 0)
        def _():
            own[i], other[i] = term[:128], term[128:]

        @pl.when(ids[0] == 1)
        def _():
            own[i], other[i] = term[128:], term[:128]


def weight_terms(ids, events, parts, after):
    width = parts.shape[1]
    shape = jax.ShapeDtypeStruct((16, 128, width), BF16)
    terms = pl.BlockSpec((4, 128, width), lambda g, _: (g, 0, 0))
    return pl.pallas_call(
        grads_kernel,
        out_shape=(shape, shape),
        grid_spec=pltpu.PrefetchScalarGridSpec(
            num_scalar_prefetch=1,
            grid=(4,),
            in_specs=[
                pl.BlockSpec((256, 1024), lambda g, _: (0, g)),
                pl.BlockSpec((256, width), lambda g, _: (0, 0)),
                pl.BlockSpec(memory_space=pl.ANY),
            ],
            out_specs=(terms, terms),
        ),
        **params(5 * 2**20, 2 * 256 * 4096 * width),
    )(ids, events, parts, after)


def back_kernel(ids, seen, own, other, out, both):
    core, x = ids[0], ids[1]
    total = jnp.zeros((256, 256), F32)
    for k in range(4):
        both[k, half(core, 0), :] = own[k]
        both[k, half(core, 1), :] = other[k]
        total = total + mt(seen[lax.rem(x + 4 - k, 4)], both[k])
    out[...] = total.astype(BF16)


def back_terms(ids, seen, own, other):
    width = seen.shape[-1]
    weights = pl.BlockSpec((4, 128, width), lambda g, _: (0, g, 0))
    return pl.pallas_call(
        back_kernel,
        out_shape=jax.ShapeDtypeStruct((256, 1024), BF16),
        grid_spec=pltpu.PrefetchScalarGridSpec(
            num_scalar_prefetch=1,
            grid=(4,),
            in_specs=[pl.BlockSpec((4, 256, width), lambda g, _: (0, 0, 0)), weights, weights],
            out_specs=pl.BlockSpec((256, 256), lambda g, _: (0, g)),
            scratch_shapes=[pltpu.VMEM((4, 256, width), BF16)],
        ),
        **params(5 * 2**20, 2 * 256 * 4096 * width),
    )(ids, seen, own, other)


def lay_kernel(pieces, out):
    out[...] = pieces[0]


def lay_out(pieces):
    return pl.pallas_call(
        lay_kernel,
        out_shape=jax.ShapeDtypeStruct((256, 4096), BF16),
        grid=(4,),
        in_specs=[pl.BlockSpec((1, 256, 1024), lambda g: (g, 0, 0))],
        out_specs=pl.BlockSpec((256, 1024), lambda g: (0, g)),
        **params(4 * 2**20, 0),
    )(pieces)


def turn(axis, k):
    return [(i, (i + k) % 4) for i in range(4)]


def on_device(events, tile_mask, initial_state, w_query, w_key, w_value, cotangent):
    core, x = lax.axis_index("core"), lax.axis_index("x")
    ids = jnp.stack((core, x)).astype(jnp.int32)
    allowed = allowed_pairs(tile_mask)
    shard = jnp.concatenate((w_query, w_key, w_value), axis=1)
    own = spread(lax.all_gather(shard, "zh"), "y")
    other = swap(own)
    projected = project(ids, events, own.reshape(16, 128, 384), other.reshape(16, 128, 384))
    queries, keys, values = (projected[:, i * 128 : (i + 1) * 128] for i in range(3))
    carried = scan_states(tm(keys, values), False, initial_state[0])

    pieces = pick(ids, own.reshape(4, 512, 384), projected)
    pieces = [pieces[0]] + [lax.ppermute(pieces[k], "x", turn("x", k)) for k in (1, 2, 3)]
    back_own = jnp.stack(pieces)
    back_other = swap(back_own)

    mixing = jnp.where(allowed, mt(queries, keys), 0.0).astype(BF16)
    mixture = mm(mixing, values) + mm(queries, carried)
    inverse_rms = lax.rsqrt(jnp.mean(mixture * mixture, axis=-1, keepdims=True) + epsilon)
    attended = (mixture * inverse_rms).astype(BF16)
    upstream = cotangent.astype(F32)
    mixture_grad = (
        inverse_rms * upstream
        - mixture * inverse_rms**3 * jnp.mean(upstream * mixture, axis=-1, keepdims=True)
    ).astype(BF16)
    later = scan_states(tm(queries, mixture_grad), True, None)
    score_grad = jnp.where(allowed, mt(mixture_grad, values), 0.0).astype(BF16)
    query_part = (mm(score_grad, keys) + mt(mixture_grad, carried)).astype(BF16)
    key_part = (tm(score_grad, queries) + mt(values, later)).astype(BF16)
    value_part = (tm(mixing, mixture_grad) + mm(keys, later)).astype(BF16)
    parts = jnp.concatenate((query_part, key_part, value_part), axis=1)

    term = back_terms(ids, spread(parts, "x"), back_own, back_other)
    summed = total(trade(term.reshape(4, 64, 1024), "zl")).astype(BF16)
    events_grad = lay_out(spread(spread(summed, "zl").reshape(256, 1024), "x"))

    mine, others = weight_terms(ids, events, parts, swap(parts[:16, :128]))
    mine = (mine.astype(F32) + swap(others).astype(F32)).astype(BF16)
    mine = lax.psum_scatter(mine.reshape(2048, 384), "y", scatter_dimension=0, tiled=True)
    pieces = mine.reshape(4, 128, 384)
    zh = lax.axis_index("zh")
    pieces = [
        lax.dynamic_index_in_dim(pieces, lax.rem(zh + k, 4), 0, keepdims=False) for k in range(4)
    ]
    pieces = [pieces[0]] + [lax.ppermute(pieces[k], "zh", turn("zh", k)) for k in (1, 2, 3)]
    grads = sum(piece.astype(F32) for piece in pieces).astype(BF16)
    return (attended, events_grad, grads[:, :128], grads[:, 128:256], grads[:, 256:])


def solution(mesh):
    fine = Mesh(mesh.devices.reshape(4, 4, 2, 4, 4), CTX + FSDP)
    both = P(CTX, FSDP)
    return jax.shard_map(
        on_device,
        mesh=fine,
        in_specs=(P(CTX, None), P(CTX, None), P(FSDP, None, None), both, both, both, both),
        out_specs=(both, P(CTX, None), both, both, both),
        check_vma=False,
    )
```

time: 374 us -> 256 us (0.68)
  waiting for transfers between devices: 155 us -> 27 us
  blocking collectives: 19.4 us -> 117 us
  starting transfers between devices: 122 us -> 57.4 us
  matrix products: 39.7 us -> 4.26 us
  Pallas kernels: 0 us -> 14 us
  local copies, waits for them, and re-layouts: 21.8 us -> 8.03 us
  between operations: 1.23 us -> 14.6 us
    all_to_all x11 -> x1, waiting for transfers between devices: 92.5 us -> 10.9 us  [trade(): return lax.all_to_all(pieces, axis, 0, 0)]
    all_gather x0 -> x3, blocking collectives: none -> 66.6 us  [the longest x2 38.8 us: scan_states(): near = lax.all_gather(local.astype(BF16), ('zh', 'core')).astype(F32)]
    all_to_all x7 -> x3, waiting for transfers between devices: 60.1 us -> 2.17 us  [spread(): lax.all_to_all(jnp.broadcast_to(array[None], (count, *array.shape)), axis...]
    all_to_all x11 -> x1, starting transfers between devices: 48.9 us -> 4.14 us  [trade(): return lax.all_to_all(pieces, axis, 0, 0)]
    dot_general x38 -> x12, matrix products: 39.7 us -> 4.26 us  [dot(): return lax.dot_general(a, b, (dims, ((), ())), preferred_element_type=F32)]
    all_to_all x7 -> x3, starting transfers between devices: 44.8 us -> 11.4 us  [spread(): lax.all_to_all(jnp.broadcast_to(array[None], (count, *array.shape)), axis...]
    all_to_all x1 -> x3, blocking collectives: 19.4 us -> 50.6 us  [spread(): lax.all_to_all(jnp.broadcast_to(array[None], (count, *array.shape)), axis...]
    ppermute x0 -> x6, starting transfers between devices: none -> 26.7 us  [the longest x3 16.2 us: on_device(): lax.ppermute(pieces[k], 'zh', turn('zh', k))]
  transfers between devices with their start and end apart: 24 -> 15, of which waited for: 16 -> 4; matrix products, arithmetic and copies ran while one was open for 15% -> 8% of each run, Pallas kernels for 0% -> 4%
where the time goes in v2:
time: 256 us; the launch traced here: 254 us
  blocking collectives  117 us (46%)
  starting transfers between devices  57.4 us (22%)
  waiting for transfers between devices  27 us (11%)
  between operations  14.6 us (6%)
  Pallas kernels  14 us (5%)
  other arithmetic  12 us (5%)
  local copies, waits for them, and re-layouts  8.03 us (3%)
  matrix products  4.26 us (2%)
    all_to_all x3, blocking collectives, spread(): lax.all_to_all(jnp.broadcast_to(array[None], (count, *array.shape)), axis...  50.6 us
    all_gather x2, blocking collectives, scan_states(): near = lax.all_gather(local.astype(BF16), ('zh', 'core')).astype(F32)  38.8 us
    all_gather x1, blocking collectives, on_device(): own = spread(lax.all_gather(shard, 'zh'), 'y')  27.8 us
    ppermute x3, starting transfers between devices, on_device(): lax.ppermute(pieces[k], 'zh', turn('zh', k))  16.2 us
    ppermute x4, starting transfers between devices, swap(): return lax.ppermute(array, 'core', SWAP)  15.1 us
    ppermute x3, waiting for transfers between devices, on_device(): lax.ppermute(pieces[k], 'zh', turn('zh', k))  13.8 us
    all_to_all x3, starting transfers between devices, spread(): lax.all_to_all(jnp.broadcast_to(array[None], (count, *array.shape)), axis...  11.4 us
    all_to_all x1, waiting for transfers between devices, trade(): return lax.all_to_all(pieces, axis, 0, 0)  10.9 us
  transfers between devices with their start and end apart: 15, of which 4 were waited for; matrix products, arithmetic and copies ran while one was open for 8% of the time, Pallas kernels for 4%

profile of v2, /device:TPU:1, one launch (start us, length us, event | category | flops | bytes accessed | tf_op | source)
XLA Modules:
  0.0 254.5 jit_solution(11378436765547358371)
XLA Ops:
  8.0 27.8 %all-gather = bf16[512,384]{1,0:T(8,128)(2,1)S(1)} all-gather(bf16[128,384]{1,0:T(8,128)(2,1)S(1)} %pad_maximum_fusion.2), channel_id=2, replica_groups=mesh['y'=4,'zh'=4,'core'=2,'zl'=4,'x'=4] {'zh'}, dimensions={0}, use_global_device_ids=true | all-gather | bytes 491520 | tf_op jit(solution)/shard_map/all_gather | solution.py:225
  36.0 20.4 %all_to_all.35 = bf16[4,4,128,384]{3,2,1,0:T(8,128)(2,1)S(1)} all-to-all(bf16[4,4,128,384]{3,2,1,0:T(8,128)(2,1)S(1)} %broadcast_in_dim.95), channel_id=1, replica_groups=mesh['y'=4,'zh'=4,'core'=2,'zl'=4,'x'=4] {'y'}, dimensions={0} | all-to-all | bytes 3145728 | tf_op jit(solution)/shard_map/all_to_all | solution.py:37
  56.4 7.3 %collective-permute-start = (bf16[4,4,128,384]{3,2,1,0:T(8,128)(2,1)S(1)}, bf16[4,4,128,384]{3,2,1,0:T(8,128)(2,1)S(1)}, u32[]{:S(2)}, u32[]{:S(2)}) collective-permute-start(bf16[4,4,128,384]{3,2,1,0:T(8,128)(2,1)S(1)} %all_to_all.35), channel_id=1, source_target_pairs={{0,16},{16,0},{1,17},{17,1},{2,18},{18,2},{3,19},{19,3},{4,20},{20... | collective-permute-start | bytes 4718600 | tf_op jit(solution)/shard_map/ppermute | solution.py:49
  65.1 1.8 iota_compare_fusion.1
  66.9 1.6 copy-done
  68.5 2.7 %shard_map.110.after = bf16[256,384]{1,0:T(8,128)(2,1)S(1)} custom-call(s32[2]{0:T(128)S(1)} %pad_add_fusion.ids, bf16[256,4096]{1,0:T(8,128)(2,1)S(1)} %copy-done, bf16[16,128,384]{2,1,0:T(8,128)(2,1)S(1)} %bitcast.46, bf16[16,128,384]{2,1,0:T(8,128)(2,1)S(1)} %bitcast.48), custom_call_target="tpu_custom_call" | custom-call | flops 805306368 | bytes 5242880 | tf_op jit(solution)/shard_map/pallas_call | solution.py:109
  71.4 19.4 %all-gather.1 = bf16[1024,128]{1,0:T(8,128)(2,1)S(1)} all-gather(bf16[128,128]{1,0:T(8,128)(2,1)S(1)} %convolution_convert_fusion.1), channel_id=3, replica_groups=mesh['y'=4,'zh'=4,'core'=2,'zl'=4,'x'=4] {'zh','core'}, dimensions={0}, use_global_device_ids=true | all-gather | bytes 294912 | tf_op jit(solution)/shard_map/all_gather | solution.py:68
  91.5 3.3 %all-to-all-start.1 = ((bf16[4,128,128]{2,1,0:T(8,128)(2,1)}), bf16[4,128,128]{2,1,0:T(8,128)(2,1)S(1)}, u32[]{:S(2)}, u32[]{:S(2)}) async-start(bf16[4,128,128]{2,1,0:T(8,128)(2,1)} %broadcast_in_dim.100), calls=%async_computation.1 | async-start | bytes 262144 | tf_op jit(solution)/shard_map/all_to_all | solution.py:37
  95.5 3.1 %collective-permute-start.1 = (bf16[512,384]{1,0:T(8,128)(2,1)S(1)}, bf16[512,384]{1,0:T(8,128)(2,1)S(1)}, u32[]{:S(2)}, u32[]{:S(2)}) collective-permute-start(bf16[512,384]{1,0:T(8,128)(2,1)S(1)} %get-tuple-element.12), channel_id=1, source_target_pairs={{0,1},{1,2},{2,3},{3,0},{4,5},{5,6},{6,7},{7,4},{8,9},{9,10},{10,1... | collective-permute-start | bytes 1179656 | tf_op jit(solution)/shard_map/ppermute | solution.py:232
  98.6 4.4 %collective-permute-start.2 = (bf16[512,384]{1,0:T(8,128)(2,1)S(1)}, bf16[512,384]{1,0:T(8,128)(2,1)}, u32[]{:S(2)}, u32[]{:S(2)}) collective-permute-start(bf16[512,384]{1,0:T(8,128)(2,1)S(1)} %get-tuple-element.13), channel_id=1, source_target_pairs={{0,2},{1,3},{2,0},{3,1},{4,6},{5,7},{6,4},{7,5},{8,10},{9,11},{10,... | collective-permute-start | bytes 1179656 | tf_op jit(solution)/shard_map/ppermute | solution.py:232
  103.0 3.0 %collective-permute-start.3 = (bf16[512,384]{1,0:T(8,128)(2,1)S(1)}, bf16[512,384]{1,0:T(8,128)(2,1)}, u32[]{:S(2)}, u32[]{:S(2)}) collective-permute-start(bf16[512,384]{1,0:T(8,128)(2,1)S(1)} %get-tuple-element.14), channel_id=1, source_target_pairs={{0,3},{1,0},{2,1},{3,2},{4,7},{5,4},{6,5},{7,6},{8,11},{9,8},{10,9... | collective-permute-start | bytes 1179656 | tf_op jit(solution)/shard_map/ppermute | solution.py:232
  111.3 19.4 %all-gather.2 = bf16[1024,128]{1,0:T(8,128)(2,1)S(1)} all-gather(bf16[128,128]{1,0:T(8,128)(2,1)S(1)} %convolution_convert_fusion), channel_id=4, replica_groups=mesh['y'=4,'zh'=4,'core'=2,'zl'=4,'x'=4] {'zh','core'}, dimensions={0}, use_global_device_ids=true | all-gather | bytes 294912 | tf_op jit(solution)/shard_map/all_gather | solution.py:68
  131.4 4.5 %all-to-all-start.2 = ((bf16[4,128,128]{2,1,0:T(8,128)(2,1)}), bf16[4,128,128]{2,1,0:T(8,128)(2,1)S(1)}, u32[]{:S(2)}, u32[]{:S(2)}) async-start(bf16[4,128,128]{2,1,0:T(8,128)(2,1)} %broadcast_in_dim.104), calls=%async_computation.2 | async-start | bytes 262144 | tf_op jit(solution)/shard_map/all_to_all | solution.py:37
  136.1 2.4 collective-permute-start.5
  138.6 2.2 all-to-all-done.2
  142.6 3.5 %collective-permute-start.4 = (bf16[4,512,384]{2,1,0:T(8,128)(2,1)S(1)}, bf16[4,512,384]{2,1,0:T(8,128)(2,1)S(1)}, u32[]{:S(2)}, u32[]{:S(2)}) collective-permute-start(bf16[4,512,384]{2,1,0:T(8,128)(2,1)S(1)} %pad_maximum_fusion.own), channel_id=1, source_target_pairs={{0,16},{16,0},{1,17},{17,1},{2,18},{18,2},{3,19},{19,3},{4,20},{20... | collective-permute-start | bytes 4718600 | tf_op jit(solution)/shard_map/ppermute | solution.py:49
  146.6 5.3 %shard_map.114 = (bf16[16,128,384]{2,1,0:T(8,128)(2,1)S(1)}, bf16[16,128,384]{2,1,0:T(8,128)(2,1)S(1)}) custom-call(s32[2]{0:T(128)S(1)} %pad_add_fusion.ids, bf16[256,4096]{1,0:T(8,128)(2,1)S(1)} %copy-done.1, bf16[256,384]{1,0:T(8,128)(2,1)S(1)} %pad_maximum_fusion.1.parts, bf16[16,128]{1,0:T(8,128)(2,1)S(1)} %collective-permute-done.5.after), custom_call_target="tpu_custom_call" | custom-call | flops 805306368 | bytes 5242880 | tf_op jit(solution)/shard_map/pallas_call | solution.py:157
  151.8 1.9 collective-permute-start.6
  153.8 14.3 %all_to_all.36.seen = bf16[4,256,384]{2,1,0:T(8,128)(2,1)S(1)} all-to-all(bf16[4,256,384]{2,1,0:T(8,128)(2,1)S(1)} %broadcast_in_dim.105), channel_id=1, replica_groups=mesh['y'=4,'zh'=4,'core'=2,'zl'=4,'x'=4] {'x'}, dimensions={0} | all-to-all | bytes 1572864 | tf_op jit(solution)/shard_map/all_to_all | solution.py:37
  168.1 3.6 %shard_map.112 = bf16[256,1024]{1,0:T(8,128)(2,1)} custom-call(s32[2]{0:T(128)S(1)} %pad_add_fusion.ids, bf16[4,256,384]{2,1,0:T(8,128)(2,1)S(1)} %all_to_all.36.seen, bf16[4,512,384]{2,1,0:T(8,128)(2,1)S(1)} %pad_maximum_fusion.own, bf16[4,512,384]{2,1,0:T(8,128)(2,1)S(1)} %collective-permute-done.4.other), custom_call_target="tpu_custom_call" | custom-call | flops 805306368 | bytes 5242880 | tf_op jit(solution)/shard_map/pallas_call | solution.py:187
  171.7 4.1 %all-to-all-start.4 = ((bf16[4,64,1024]{2,1,0:T(8,128)(2,1)}), bf16[4,64,1024]{2,1,0:T(8,128)(2,1)}, u32[]{:S(2)}, u32[]{:S(2)}) async-start(bf16[4,64,1024]{2,1,0:T(8,128)(2,1)} %bitcast.16), calls=%async_computation.4 | async-start | bytes 1048576 | tf_op jit(solution)/shard_map/all_to_all | solution.py:41
  175.9 3.1 %add_convert_fusion = bf16[16,128,384]{2,1,0:T(8,128)(2,1)} fusion(bf16[16,128,384]{2,1,0:T(8,128)(2,1)} %collective-permute-done.6, bf16[16,128,384]{2,1,0:T(8,128)(2,1)S(1)} %get-tuple-element.15), kind=kLoop, calls=%fused_computation | loop fusion | flops 3145728 | bytes 4718592 | tf_op jit(solution)/shard_map/convert_element_type | solution.py:257
  179.0 10.9 %all-to-all-done.4 = bf16[4,64,1024]{2,1,0:T(8,128)(2,1)} async-done(((bf16[4,64,1024]{2,1,0:T(8,128)(2,1)}), bf16[4,64,1024]{2,1,0:T(8,128)(2,1)}, u32[]{:S(2)}, u32[]{:S(2)}) %all-to-all-start.4) | async-done | bytes 524320 | tf_op jit(solution)/shard_map/all_to_all | solution.py:41
  191.1 16.0 %all_to_all.37 = bf16[4,64,1024]{2,1,0:T(8,128)(2,1)S(1)} all-to-all(bf16[4,64,1024]{2,1,0:T(8,128)(2,1)S(1)} %broadcast_in_dim.106), channel_id=1, replica_groups=mesh['y'=4,'zh'=4,'core'=2,'zl'=4,'x'=4] {'zl'}, dimensions={0} | all-to-all | bytes 1048576 | tf_op jit(solution)/shard_map/all_to_all | solution.py:37
  207.1 1.6 broadcast_in_dim.108
  208.7 3.6 %all-to-all-start.6 = ((bf16[4,256,1024]{2,1,0:T(8,128)(2,1)}), bf16[4,256,1024]{2,1,0:T(8,128)(2,1)S(1)}, u32[]{:S(2)}, u32[]{:S(2)}) async-start(bf16[4,256,1024]{2,1,0:T(8,128)(2,1)} %broadcast_in_dim.108), calls=%async_computation.6 | async-start | bytes 4194304 | tf_op jit(solution)/shard_map/all_to_all | solution.py:37
  213.4 3.6 %collective-permute-start.7 = (bf16[128,384]{1,0:T(8,128)(2,1)S(1)}, bf16[128,384]{1,0:T(8,128)(2,1)S(1)}, u32[]{:S(2)}, u32[]{:S(2)}) collective-permute-start(bf16[128,384]{1,0:T(8,128)(2,1)S(1)} %get-tuple-element.29), channel_id=1, source_target_pairs={{0,32},{32,64},{64,96},{96,0},{1,33},{33,65},{65,97},{97,1},{2,34}... | collective-permute-start | bytes 294920 | tf_op jit(solution)/shard_map/ppermute | solution.py:264
  217.0 7.0 %collective-permute-start.8 = (bf16[128,384]{1,0:T(8,128)(2,1)S(1)}, bf16[128,384]{1,0:T(8,128)(2,1)S(1)}, u32[]{:S(2)}, u32[]{:S(2)}) collective-permute-start(bf16[128,384]{1,0:T(8,128)(2,1)S(1)} %get-tuple-element.31), channel_id=1, source_target_pairs={{0,64},{32,96},{64,0},{96,32},{1,65},{33,97},{65,1},{97,33},{2,66}... | collective-permute-start | bytes 294920 | tf_op jit(solution)/shard_map/ppermute | solution.py:264
  224.0 5.6 %collective-permute-start.9 = (bf16[128,384]{1,0:T(8,128)(2,1)S(1)}, bf16[128,384]{1,0:T(8,128)(2,1)S(1)}, u32[]{:S(2)}, u32[]{:S(2)}) collective-permute-start(bf16[128,384]{1,0:T(8,128)(2,1)S(1)} %get-tuple-element.30), channel_id=1, source_target_pairs={{0,96},{32,0},{64,32},{96,64},{1,97},{33,1},{65,33},{97,65},{2,98}... | collective-permute-start | bytes 294920 | tf_op jit(solution)/shard_map/ppermute | solution.py:264
  230.3 5.8 %collective-permute-done.8 = bf16[128,384]{1,0:T(8,128)(2,1)S(1)} collective-permute-done((bf16[128,384]{1,0:T(8,128)(2,1)S(1)}, bf16[128,384]{1,0:T(8,128)(2,1)S(1)}, u32[]{:S(2)}, u32[]{:S(2)}) %collective-permute-start.8) | collective-permute-done | bytes 98336 | tf_op jit(solution)/shard_map/ppermute | solution.py:264
  236.2 8.0 %collective-permute-done.9 = bf16[128,384]{1,0:T(8,128)(2,1)S(1)} collective-permute-done((bf16[128,384]{1,0:T(8,128)(2,1)S(1)}, bf16[128,384]{1,0:T(8,128)(2,1)S(1)}, u32[]{:S(2)}, u32[]{:S(2)}) %collective-permute-start.9) | collective-permute-done | bytes 98336 | tf_op jit(solution)/shard_map/ppermute | solution.py:264
  245.8 1.8 shard_map.113
  (74 shorter events, 17.0 us)
Async XLA Ops:
  36.0 27.7 %copy-start.4 = (bf16[256,128]{1,0:T(8,128)(2,1)S(1)}, bf16[256,128]{1,0:T(8,128)(2,1)}, u32[]{:S(2)}) copy-start(bf16[256,128]{1,0:T(8,128)(2,1)} %param.13) | copy-start | bytes 196612
  36.0 28.5 %copy-start.7 = (s32[2,2]{1,0:T(2,128)S(1)}, s32[2,2]{1,0:T(2,128)}, u32[]{:S(2)}) copy-start(s32[2,2]{1,0:T(2,128)} %param.8) | copy-start | bytes 52
  56.4 10.5 %collective-permute-start = (bf16[4,4,128,384]{3,2,1,0:T(8,128)(2,1)S(1)}, bf16[4,4,128,384]{3,2,1,0:T(8,128)(2,1)S(1)}, u32[]{:S(2)}, u32[]{:S(2)}) collective-permute-start(bf16[4,4,128,384]{3,2,1,0:T(8,128)(2,1)S(1)} %all_to_all.35), channel_id=1, source_target_pairs={{0,16},{16,0},{1,17},{17,1},{2,18},{18,2},{3,19},{19,3},{4,20},{20... | collective-permute-start | bytes 4718600 | tf_op jit(solution)/shard_map/ppermute | solution.py:49
  66.9 1.6 copy-start
  90.7 4.1 %copy-start.2 = (bf16[1024,128]{1,0:T(8,128)(2,1)}, bf16[1024,128]{1,0:T(8,128)(2,1)S(1)}, u32[]{:S(2)}) copy-start(bf16[1024,128]{1,0:T(8,128)(2,1)S(1)} %all-gather.1) | copy-start | bytes 786436
  91.5 16.9 %all-to-all-start.1 = ((bf16[4,128,128]{2,1,0:T(8,128)(2,1)}), bf16[4,128,128]{2,1,0:T(8,128)(2,1)S(1)}, u32[]{:S(2)}, u32[]{:S(2)}) async-start(bf16[4,128,128]{2,1,0:T(8,128)(2,1)} %broadcast_in_dim.100), calls=%async_computation.1 | async-start | bytes 262144 | tf_op jit(solution)/shard_map/all_to_all | solution.py:37
  94.8 12.7 %copy-start.3 = (bf16[1024,128]{1,0:T(8,128)(2,1)S(1)}, bf16[1024,128]{1,0:T(8,128)(2,1)}, u32[]{:S(2)}) copy-start(bf16[1024,128]{1,0:T(8,128)(2,1)} %copy-done.2) | copy-start | bytes 786436
  95.5 14.5 %copy-start.5 = (pred[256]{0:T(512)(128)(4,1)S(1)}, pred[256]{0:T(512)(128)(4,1)}, u32[]{:S(2)}) copy-start(pred[256]{0:T(512)(128)(4,1)} %get-tuple-element.43) | copy-start | bytes 772
  95.5 14.5 %copy-start.6 = (pred[256]{0:T(512)(128)(4,1)S(1)}, pred[256]{0:T(512)(128)(4,1)}, u32[]{:S(2)}) copy-start(pred[256]{0:T(512)(128)(4,1)} %get-tuple-element.44) | copy-start | bytes 772
  95.5 45.5 %collective-permute-start.1 = (bf16[512,384]{1,0:T(8,128)(2,1)S(1)}, bf16[512,384]{1,0:T(8,128)(2,1)S(1)}, u32[]{:S(2)}, u32[]{:S(2)}) collective-permute-start(bf16[512,384]{1,0:T(8,128)(2,1)S(1)} %get-tuple-element.12), channel_id=1, source_target_pairs={{0,1},{1,2},{2,3},{3,0},{4,5},{5,6},{6,7},{7,4},{8,9},{9,10},{10,1... | collective-permute-start | bytes 1179656 | tf_op jit(solution)/shard_map/ppermute | solution.py:232
  98.6 42.4 %collective-permute-start.2 = (bf16[512,384]{1,0:T(8,128)(2,1)S(1)}, bf16[512,384]{1,0:T(8,128)(2,1)}, u32[]{:S(2)}, u32[]{:S(2)}) collective-permute-start(bf16[512,384]{1,0:T(8,128)(2,1)S(1)} %get-tuple-element.13), channel_id=1, source_target_pairs={{0,2},{1,3},{2,0},{3,1},{4,6},{5,7},{6,4},{7,5},{8,10},{9,11},{10,... | collective-permute-start | bytes 1179656 | tf_op jit(solution)/shard_map/ppermute | solution.py:232
  103.0 38.0 %collective-permute-start.3 = (bf16[512,384]{1,0:T(8,128)(2,1)S(1)}, bf16[512,384]{1,0:T(8,128)(2,1)}, u32[]{:S(2)}, u32[]{:S(2)}) collective-permute-start(bf16[512,384]{1,0:T(8,128)(2,1)S(1)} %get-tuple-element.14), channel_id=1, source_target_pairs={{0,3},{1,0},{2,1},{3,2},{4,7},{5,4},{6,5},{7,6},{8,11},{9,8},{10,9... | collective-permute-start | bytes 1179656 | tf_op jit(solution)/shard_map/ppermute | solution.py:232
  131.4 9.3 %all-to-all-start.2 = ((bf16[4,128,128]{2,1,0:T(8,128)(2,1)}), bf16[4,128,128]{2,1,0:T(8,128)(2,1)S(1)}, u32[]{:S(2)}, u32[]{:S(2)}) async-start(bf16[4,128,128]{2,1,0:T(8,128)(2,1)} %broadcast_in_dim.104), calls=%async_computation.2 | async-start | bytes 262144 | tf_op jit(solution)/shard_map/all_to_all | solution.py:37
  136.1 10.4 %collective-permute-start.5 = (bf16[16,128]{1,0:T(8,128)(2,1)S(1)}, bf16[16,128]{1,0:T(8,128)(2,1)S(1)}, u32[]{:S(2)}, u32[]{:S(2)}) collective-permute-start(bf16[16,128]{1,0:T(8,128)(2,1)S(1)} %slice.43), channel_id=1, source_target_pairs={{0,16},{16,0},{1,17},{17,1},{2,18},{18,2},{3,19},{19,3},{4,20},{20... | collective-permute-start | bytes 12296 | tf_op jit(solution)/shard_map/ppermute | solution.py:49
  141.1 5.5 %copy-start.1 = (bf16[256,4096]{1,0:T(8,128)(2,1)S(1)}, bf16[256,4096]{1,0:T(8,128)(2,1)}, u32[]{:S(2)}) copy-start(bf16[256,4096]{1,0:T(8,128)(2,1)} %events.3) | copy-start | bytes 6291460
  142.6 25.6 %collective-permute-start.4 = (bf16[4,512,384]{2,1,0:T(8,128)(2,1)S(1)}, bf16[4,512,384]{2,1,0:T(8,128)(2,1)S(1)}, u32[]{:S(2)}, u32[]{:S(2)}) collective-permute-start(bf16[4,512,384]{2,1,0:T(8,128)(2,1)S(1)} %pad_maximum_fusion.own), channel_id=1, source_target_pairs={{0,16},{16,0},{1,17},{17,1},{2,18},{18,2},{3,19},{19,3},{4,20},{20... | collective-permute-start | bytes 4718600 | tf_op jit(solution)/shard_map/ppermute | solution.py:49
  151.8 24.1 %collective-permute-start.6 = (bf16[16,128,384]{2,1,0:T(8,128)(2,1)S(1)}, bf16[16,128,384]{2,1,0:T(8,128)(2,1)}, u32[]{:S(2)}, u32[]{:S(2)}) collective-permute-start(bf16[16,128,384]{2,1,0:T(8,128)(2,1)S(1)} %get-tuple-element.16), channel_id=1, source_target_pairs={{0,16},{16,0},{1,17},{17,1},{2,18},{18,2},{3,19},{19,3},{4,20},{20... | collective-permute-start | bytes 4718600 | tf_op jit(solution)/shard_map/ppermute | solution.py:49
  171.7 18.2 %all-to-all-start.4 = ((bf16[4,64,1024]{2,1,0:T(8,128)(2,1)}), bf16[4,64,1024]{2,1,0:T(8,128)(2,1)}, u32[]{:S(2)}, u32[]{:S(2)}) async-start(bf16[4,64,1024]{2,1,0:T(8,128)(2,1)} %bitcast.16), calls=%async_computation.4 | async-start | bytes 1048576 | tf_op jit(solution)/shard_map/all_to_all | solution.py:41
  175.9 36.5 %reduce-scatter.2.cloned.1.call-start = ((), (), s32[]{:S(2)}) async-start(), calls=%async_computation.8 | async-start | bytes 1966080 | tf_op jit(solution)/shard_map/reduce_scatter | solution.py:258
  208.7 37.1 %all-to-all-start.6 = ((bf16[4,256,1024]{2,1,0:T(8,128)(2,1)}), bf16[4,256,1024]{2,1,0:T(8,128)(2,1)S(1)}, u32[]{:S(2)}, u32[]{:S(2)}) async-start(bf16[4,256,1024]{2,1,0:T(8,128)(2,1)} %broadcast_in_dim.108), calls=%async_computation.6 | async-start | bytes 4194304 | tf_op jit(solution)/shard_map/all_to_all | solution.py:37
  213.4 17.0 %collective-permute-start.7 = (bf16[128,384]{1,0:T(8,128)(2,1)S(1)}, bf16[128,384]{1,0:T(8,128)(2,1)S(1)}, u32[]{:S(2)}, u32[]{:S(2)}) collective-permute-start(bf16[128,384]{1,0:T(8,128)(2,1)S(1)} %get-tuple-element.29), channel_id=1, source_target_pairs={{0,32},{32,64},{64,96},{96,0},{1,33},{33,65},{65,97},{97,1},{2,34}... | collective-permute-start | bytes 294920 | tf_op jit(solution)/shard_map/ppermute | solution.py:264
  217.0 19.2 %collective-permute-start.8 = (bf16[128,384]{1,0:T(8,128)(2,1)S(1)}, bf16[128,384]{1,0:T(8,128)(2,1)S(1)}, u32[]{:S(2)}, u32[]{:S(2)}) collective-permute-start(bf16[128,384]{1,0:T(8,128)(2,1)S(1)} %get-tuple-element.31), channel_id=1, source_target_pairs={{0,64},{32,96},{64,0},{96,32},{1,65},{33,97},{65,1},{97,33},{2,66}... | collective-permute-start | bytes 294920 | tf_op jit(solution)/shard_map/ppermute | solution.py:264
  224.0 20.2 %collective-permute-start.9 = (bf16[128,384]{1,0:T(8,128)(2,1)S(1)}, bf16[128,384]{1,0:T(8,128)(2,1)S(1)}, u32[]{:S(2)}, u32[]{:S(2)}) collective-permute-start(bf16[128,384]{1,0:T(8,128)(2,1)S(1)} %get-tuple-element.30), channel_id=1, source_target_pairs={{0,96},{32,0},{64,32},{96,64},{1,97},{33,1},{65,33},{97,65},{2,98}... | collective-permute-start | bytes 294920 | tf_op jit(solution)/shard_map/ppermute | solution.py:264
Sparse Core Ops, SparseCore 0:
  179.6 25.7 reduce-scatter.1

commit v3 on v1

v3 whole, which is shorter than its diff:
```python
import jax
import jax.numpy as jnp
from jax import lax
from jax.experimental import pallas as pl
from jax.experimental.pallas import tpu as pltpu
from jax.sharding import Mesh
from jax.sharding import PartitionSpec as P

TILE = 128
CTX = ("y", "zh", "core")
FSDP = ("zl", "x")
BF16, F32 = jnp.bfloat16, jnp.float32
CORE, X, Y, ZH = range(4)

epsilon = 1e-06


def dot(a, b, dims):
    return lax.dot_general(a, b, (dims, ((), ())), preferred_element_type=F32)


def mm(a, b):
    return dot(a, b, ((1,), (0,)))


def mt(a, b):
    return dot(a, b, ((1,), (1,)))


def tm(a, b):
    return dot(a, b, ((0,), (0,)))


def shape(*dims, dtype=BF16):
    return jax.ShapeDtypeStruct(dims, dtype)


def spread(array, axis):
    count = lax.axis_size(axis)
    return lax.all_to_all(jnp.broadcast_to(array[None], (count, *array.shape)), axis, 0, 0)


def trade(pieces, axis):
    return lax.all_to_all(pieces, axis, 0, 0)


def swap(array):
    return lax.ppermute(array, "core", ((0, 1), (1, 0)))


def shift(piece, axis, k):
    return lax.ppermute(piece, axis, [(i, (i + k) % 4) for i in range(4)])


def turn(pieces, axis):
    return [pieces[0]] + [shift(pieces[k], axis, k) for k in (1, 2, 3)]


def params(data_bytes, flops=0, mib=24):
    return dict(
        compiler_params=pltpu.CompilerParams(vmem_limit_bytes=mib * 2**20),
        cost_estimate=pl.CostEstimate(flops=flops, bytes_accessed=data_bytes, transcendentals=0),
    )


VMEM = pl.BlockSpec(memory_space=pltpu.VMEM)
SMEM = pl.BlockSpec(memory_space=pltpu.SMEM)
ANY = pl.BlockSpec(memory_space=pl.ANY)


def half(core, base=0):
    return pl.ds(pl.multiple_of(base + core * 128, 128), 128)


def columns_kernel(ids, events, own, other, own_turned, other_turned):
    for i in range(4):
        place = slice(i * 128, (i + 1) * 128)
        for core, out, turned in ((0, own, own_turned), (1, other, other_turned)):
            core = ids[CORE] if core == 0 else 1 - ids[CORE]
            block = events[:, half(core, i * 256)]
            out[:, place] = block
            turned[place, :] = block.T


def columns(ids, events):
    wide = pl.BlockSpec((256, 512), lambda g, _: (0, g))
    tall = pl.BlockSpec((512, 256), lambda g, _: (g, 0))
    return pl.pallas_call(
        columns_kernel,
        out_shape=[shape(256, 2048)] * 2 + [shape(2048, 256)] * 2,
        grid_spec=pltpu.PrefetchScalarGridSpec(
            num_scalar_prefetch=1,
            grid=(4,),
            in_specs=[pl.BlockSpec((256, 1024), lambda g, _: (0, g))],
            out_specs=[wide, wide, tall, tall],
        ),
        **params(6 * 2**20),
    )(ids, events)


def project_kernel(own_events, other_events, own, other, rows, state):
    total = mm(own_events[...], own[...]) + mm(other_events[...], other[...])
    rows[...] = total.astype(BF16)
    state[...] = tm(rows[:, 128:256], rows[:, 256:]).astype(BF16)


def project(own_events, other_events, own, other):
    width = own.shape[-1]
    return pl.pallas_call(
        project_kernel,
        out_shape=(shape(256, width), shape(128, 128)),
        in_specs=[VMEM] * 4,
        out_specs=(VMEM, VMEM),
        **params(5 * 2**20, 2 * 256 * 4096 * width),
    )(own_events, other_events, own, other)


def pick(ids, own, after, shifts):
    def kernel(ids, own, after, *refs):
        pieces, sems = refs[:-1], refs[-1]
        moves = [
            pltpu.make_async_copy(own.at[lax.rem(ids[X] + k, 4)], piece, sems.at[i])
            for i, (k, piece) in enumerate(zip(shifts, pieces))
        ]
        for move in moves:
            move.start()
        for move in moves:
            move.wait()

    return pl.pallas_call(
        kernel,
        out_shape=[shape(*own.shape[1:])] * len(shifts),
        in_specs=[SMEM, ANY, ANY],
        out_specs=[ANY] * len(shifts),
        scratch_shapes=[pltpu.SemaphoreType.DMA((len(shifts),))],
        **params(3 * 2**20),
    )(ids, own, after)


def join_kernel(a, b, c, d, after, out, sems):
    moves = [
        pltpu.make_async_copy(piece, out.at[k], sems.at[k]) for k, piece in enumerate((a, b, c, d))
    ]
    for move in moves:
        move.start()
    for move in moves:
        move.wait()


def join(pieces, after):
    return pl.pallas_call(
        join_kernel,
        out_shape=shape(4, *pieces[0].shape),
        in_specs=[ANY] * 5,
        out_specs=ANY,
        scratch_shapes=[pltpu.SemaphoreType.DMA((4,))],
        **params(3 * 2**20),
    )(*pieces, after)


def prefix_kernel(reverse, ids, near, *refs):
    out, y = refs[-1], ids[Y]
    chip = ids[ZH] * 2 + ids[CORE]
    before = jnp.zeros((128, 128), F32) if reverse else refs[0][0]
    line = jnp.zeros((128, 128), F32)
    for i in range(8):
        term = near[i].astype(F32)
        line = line + term
        before = before + jnp.where(i > chip if reverse else i < chip, term, 0.0)
    for to in range(4):
        sent = jnp.where(y > to if reverse else y < to, line, 0.0)
        sent = jnp.where(y == to, before, sent).astype(BF16)
        if reverse:
            for x in range(4):
                out[to, x] = sent
        else:
            out[to] = sent


def prefix_terms(ids, near, entering=None):
    reverse = entering is None
    dims = (4, 4, 128, 128) if reverse else (4, 128, 128)
    return pl.pallas_call(
        lambda *refs: prefix_kernel(reverse, *refs),
        out_shape=shape(*dims),
        in_specs=[SMEM, VMEM] + [VMEM] * (not reverse),
        out_specs=VMEM,
        **params(2**20),
    )(ids, near, *(() if reverse else (entering,)))


def allowed_pairs(mask):
    row = lax.broadcasted_iota(jnp.int32, (2 * TILE, 2 * TILE), 0)
    col = lax.broadcasted_iota(jnp.int32, (2 * TILE, 2 * TILE), 1)
    lower = jnp.where(col < TILE, mask[1, 0], mask[1, 1])
    return (col <= row) & (jnp.where(row < TILE, mask[0, 0], lower) > 0)


def mix_kernel(mask, rows, mixing, within):
    queries, keys, values = (rows[:, i * 128 : (i + 1) * 128] for i in range(3))
    mixed = jnp.where(allowed_pairs(mask), mt(queries, keys), 0.0).astype(BF16)
    mixing[...] = mixed
    within[...] = mm(mixed, values)


def mix(mask, rows):
    return pl.pallas_call(
        mix_kernel,
        out_shape=(shape(256, 256), shape(256, 128, dtype=F32)),
        in_specs=[SMEM, VMEM],
        out_specs=(VMEM, VMEM),
        **params(2**20, 2 * 256 * 256 * 256),
    )(mask, rows)


def middle_kernel(mask, rows, mixing, within, states, cotangent, attended, early, local_grad):
    queries, keys, values = (rows[:, i * 128 : (i + 1) * 128] for i in range(3))
    carried = jnp.sum(states[...].astype(F32), axis=0).astype(BF16)
    mixture = within[...] + mm(queries, carried)
    inverse_rms = lax.rsqrt(jnp.mean(mixture * mixture, axis=-1, keepdims=True) + epsilon)
    attended[...] = (mixture * inverse_rms).astype(BF16)
    upstream = cotangent[...].astype(F32)
    mixture_grad = (
        inverse_rms * upstream
        - mixture * inverse_rms**3 * jnp.mean(upstream * mixture, axis=-1, keepdims=True)
    ).astype(BF16)
    local_grad[...] = tm(queries, mixture_grad).astype(BF16)
    score_grad = jnp.where(allowed_pairs(mask), mt(mixture_grad, values), 0.0).astype(BF16)
    early[:, :128] = (mm(score_grad, keys) + mt(mixture_grad, carried)).astype(BF16)
    early[:, 128:256] = tm(score_grad, queries).astype(BF16)
    early[:, 256:384] = tm(mixing[...], mixture_grad).astype(BF16)
    early[:, 384:] = rows[:, 128:]


def middle(mask, rows, mixing, within, states, cotangent):
    return pl.pallas_call(
        middle_kernel,
        out_shape=(shape(256, 128), shape(256, 640), shape(128, 128)),
        in_specs=[SMEM] + [VMEM] * 5,
        out_specs=(VMEM,) * 3,
        **params(2**20, 2**28),
    )(mask, rows, mixing, within, states, cotangent)


def finish(early, later, out):
    keys, values = early[:, 384:512], early[:, 512:]
    out[:, :128] = early[:, :128]
    out[:, 128:256] = (early[:, 128:256].astype(F32) + mt(values, later)).astype(BF16)
    out[:, 256:] = (early[:, 256:384].astype(F32) + mm(keys, later)).astype(BF16)


def later_state(states, x):
    return sum(states[y, x].astype(F32) for y in range(4)).astype(BF16)


def parts_kernel(ids, early, states, after, out):
    finish(early, later_state(states, ids[X]), out)


def own_parts(ids, early, states, after):
    return pl.pallas_call(
        parts_kernel,
        out_shape=shape(256, 384),
        in_specs=[SMEM, VMEM, VMEM, ANY],
        out_specs=VMEM,
        **params(2**20, 2**25),
    )(ids, early, states, after)


def back_kernel(ids, early, states, own, other, after, out, *scratch):
    core, x = ids[CORE], ids[X]
    parts, heads, mine, others, sems = scratch
    moves = [pltpu.make_async_copy(early.at[j], heads.at[j], sems.at[j]) for j in range(4)]
    moves.append(pltpu.make_async_copy(own, mine, sems.at[4]))
    moves.append(pltpu.make_async_copy(other, others, sems.at[5]))
    for move in moves:
        move.start()
    for j in range(4):
        moves[j].wait()
        finish(heads.at[j], later_state(states, j), parts.at[j])
    for i, place, weights in ((4, core, mine), (5, 1 - core, others)):
        moves[i].wait()
        total = sum(mt(parts[lax.rem(x + 4 - k, 4)], weights[k]) for k in range(4)).astype(BF16)
        for i in range(4):
            out[:, half(place, i * 256)] = total[:, i * 128 : (i + 1) * 128]


def back_terms(ids, early, states, own, other, after):
    return pl.pallas_call(
        back_kernel,
        out_shape=shape(256, 1024),
        in_specs=[SMEM, ANY, VMEM, ANY, ANY, ANY],
        out_specs=VMEM,
        scratch_shapes=[
            pltpu.VMEM((4, 256, 384), BF16),
            pltpu.VMEM((4, 256, 640), BF16),
            pltpu.VMEM((4, 512, 384), BF16),
            pltpu.VMEM((4, 512, 384), BF16),
            pltpu.SemaphoreType.DMA((6,)),
        ],
        **params(5 * 2**20, 2 * 256 * 4096 * 384),
    )(ids, early, states, own, other, after)


def grads_kernel(events, crossed, parts, other, out):
    for k in range(4):
        rows = slice(k * 512, (k + 1) * 512)
        term = mm(events[rows, :], parts[...]) + mm(crossed[rows, :], other[...])
        out[rows, :] = term.astype(BF16)


def weight_terms(events, crossed, parts, other):
    width = parts.shape[1]
    return pl.pallas_call(
        grads_kernel,
        out_shape=shape(2048, width),
        in_specs=[VMEM] * 4,
        out_specs=VMEM,
        **params(5 * 2**20, 2 * 256 * 4096 * width),
    )(events, crossed, parts, other)


def regroup_kernel(ids, grads, *pieces):
    for k in range(4):
        rows = pl.ds(pl.multiple_of(lax.rem(ids[ZH] + k, 4) * 128, 128), 128)
        pieces[k][...] = grads[rows, :]


def regroup(ids, grads):
    return pl.pallas_call(
        regroup_kernel,
        out_shape=[shape(128, 384)] * 4,
        in_specs=[SMEM, VMEM],
        out_specs=[VMEM] * 4,
        **params(2 * 2**20),
    )(ids, grads)


def sum_kernel(pieces, *refs):
    out = refs[-1]
    summed = sum(pieces[k].astype(F32) for k in range(4)).astype(BF16)
    for k in range(4):
        out[k] = summed


def summed_for_all(pieces, *after):
    return pl.pallas_call(
        sum_kernel,
        out_shape=shape(*pieces.shape),
        in_specs=[VMEM] + [ANY] * len(after),
        out_specs=VMEM,
        **params(2**20),
    )(pieces, *after)


def lay_kernel(pieces, out):
    out[...] = pieces[0]


def lay_out(pieces):
    return pl.pallas_call(
        lay_kernel,
        out_shape=shape(256, 4096),
        grid=(4,),
        in_specs=[pl.BlockSpec((1, 256, 1024), lambda g: (g, 0, 0))],
        out_specs=pl.BlockSpec((256, 1024), lambda g: (0, g)),
        **params(4 * 2**20),
    )(pieces)


def on_device(events, tile_mask, initial_state, w_query, w_key, w_value, cotangent):
    ids = jnp.stack([lax.axis_index(axis) for axis in ("core", "x", "y", "zh")]).astype(jnp.int32)
    shard = jnp.concatenate((w_query, w_key, w_value), axis=1)
    own = spread(lax.all_gather(shard, "zh"), "y").reshape(2048, 384)
    own_events, other_events, own_turned, other_turned = columns(ids, events)
    rows, local_state = project(own_events, other_events, own, swap(own))

    near = lax.all_gather(local_state, ("zh", "core"))
    states = trade(prefix_terms(ids, near, initial_state), "y")
    mixing, within = mix(tile_mask, rows)
    quarters = own.reshape(4, 512, 384)
    back = turn(pick(ids, quarters, near, range(4)), "x")

    attended, early, local_grad = middle(tile_mask, rows, mixing, within, states, cotangent)
    heads = lax.all_gather(early, "x")
    near = lax.all_gather(local_grad, ("zh", "core"))
    sent = prefix_terms(ids, near).reshape(16, 128, 128)
    back_own = join(back, sent)
    back_other = swap(back_own)
    crossed = swap(other_turned)
    states = trade(sent, ("y", "x")).reshape(4, 4, 128, 128)
    parts = own_parts(ids, early, states, crossed)

    grads = weight_terms(own_turned, crossed, parts, swap(parts))
    term = back_terms(ids, heads, states, back_own, back_other, grads)
    summed = summed_for_all(trade(term.reshape(4, 64, 1024), "zl"))
    gathered = trade(summed, "zl").reshape(256, 1024)
    events_grad = lay_out(spread(gathered, "x"))
    grads = lax.psum_scatter(grads, "y", scatter_dimension=0, tiled=True)
    pieces = turn(regroup(ids, grads), "zh")
    grads = sum(piece.astype(F32) for piece in pieces).astype(BF16)
    return (attended, events_grad, grads[:, :128], grads[:, 128:256], grads[:, 256:])


def solution(mesh):
    fine = Mesh(mesh.devices.reshape(4, 4, 2, 4, 4), CTX + FSDP)
    both = P(CTX, FSDP)
    return jax.shard_map(
        on_device,
        mesh=fine,
        in_specs=(P(CTX, None), P(CTX, None), P(FSDP, None, None), both, both, both, both),
        out_specs=(both, P(CTX, None), both, both, both),
        check_vma=False,
    )
```

time: 374 us -> 251 us (0.67); the launches traced: 369 us -> 250 us
  waiting for transfers between devices: 155 us -> 40.5 us
  blocking collectives: 19.4 us -> 103 us
  starting transfers between devices: 122 us -> 57.2 us
  matrix products: 39.7 us -> 0 us
  Pallas kernels: 0 us -> 23 us
  between operations: 1.23 us -> 15.8 us
  local copies, waits for them, and re-layouts: 21.8 us -> 9.78 us
  other arithmetic: 9.84 us -> 0.94 us
    all_to_all x11 -> x3, waiting for transfers between devices: 92.5 us -> 24.5 us  [trade(): return lax.all_to_all(pieces, axis, 0, 0)]
    all_gather x0 -> x3, blocking collectives: none -> 66.7 us  [the longest x1 27.8 us: on_device(): own = spread(lax.all_gather(shard, 'zh'), 'y').reshape(2048, 384)]
    all_to_all x7 -> x1, waiting for transfers between devices: 60.1 us -> 0.01 us  [spread(): lax.all_to_all(jnp.broadcast_to(array[None], (count, *array.shape)), axis...]
    all_to_all x7 -> x1, starting transfers between devices: 44.8 us -> 3.61 us  [spread(): lax.all_to_all(jnp.broadcast_to(array[None], (count, *array.shape)), axis...]
    dot_general x38 -> x0, matrix products: 39.7 us -> none  [dot(): return lax.dot_general(a, b, (dims, ((), ())), preferred_element_type=F32)]
    all_to_all x11 -> x3, starting transfers between devices: 48.9 us -> 11.4 us  [trade(): return lax.all_to_all(pieces, axis, 0, 0)]
    pallas_call x0 -> x14, Pallas kernels: none -> 23 us  [the longest x1 4.29 us: back_terms(): pl.pallas_call(back_kernel, out_shape=shape(256, 1024), in_specs=[SMEM, A...]
    all_to_all x0 -> x1, blocking collectives: none -> 16 us  [trade(): return lax.all_to_all(pieces, axis, 0, 0)]
  transfers between devices with their start and end apart: 24 -> 16, of which waited for: 16 -> 5; matrix products, arithmetic and copies ran while one was open for 15% -> 1% of each run, Pallas kernels for 0% -> 6%
where the time goes in v3:
time: 251 us; the launch traced here: 250 us
  blocking collectives  103 us (41%)
  starting transfers between devices  57.2 us (23%)
  waiting for transfers between devices  40.5 us (16%)
  Pallas kernels  23 us (9%)
  between operations  15.8 us (6%)
  local copies, waits for them, and re-layouts  9.78 us (4%)
    all_gather x1, blocking collectives, on_device(): own = spread(lax.all_gather(shard, 'zh'), 'y').reshape(2048, 384)  27.8 us
    ppermute x6, starting transfers between devices, shift(): return lax.ppermute(piece, axis, [(i, (i + k) % 4) for i in range(4)])  27 us
    all_to_all x3, waiting for transfers between devices, trade(): return lax.all_to_all(pieces, axis, 0, 0)  24.5 us
    all_to_all x1, blocking collectives, spread(): lax.all_to_all(jnp.broadcast_to(array[None], (count, *array.shape)), axis...  20.2 us
    all_gather x1, blocking collectives, on_device(): near = lax.all_gather(local_state, ('zh', 'core'))  19.5 us
    all_gather x1, blocking collectives, on_device(): near = lax.all_gather(local_grad, ('zh', 'core'))  19.4 us
    all_to_all x1, blocking collectives, trade(): return lax.all_to_all(pieces, axis, 0, 0)  16 us
    ppermute x4, starting transfers between devices, swap(): return lax.ppermute(array, 'core', ((0, 1), (1, 0)))  15.1 us
  transfers between devices with their start and end apart: 16, of which 5 were waited for; matrix products, arithmetic and copies ran while one was open for 1% of the time, Pallas kernels for 6%

profile of v3, /device:TPU:1, one launch (start us, length us, event | category | flops | bytes accessed | tf_op | source)
XLA Modules:
  0.0 250.1 jit_solution(1289068838139032260)
XLA Ops:
  8.8 27.8 %all-gather = bf16[512,384]{1,0:T(8,128)(2,1)S(1)} all-gather(bf16[128,384]{1,0:T(8,128)(2,1)S(1)} %pad_maximum_fusion), channel_id=2, replica_groups=mesh['y'=4,'zh'=4,'core'=2,'zl'=4,'x'=4] {'zh'}, dimensions={0}, use_global_device_ids=true | all-gather | bytes 491520 | tf_op jit(solution)/shard_map/all_gather | solution.py:374
  36.8 20.2 %all_to_all.30 = bf16[4,4,128,384]{3,2,1,0:T(8,128)(2,1)S(1)} all-to-all(bf16[4,4,128,384]{3,2,1,0:T(8,128)(2,1)S(1)} %broadcast_in_dim.6), channel_id=1, replica_groups=mesh['y'=4,'zh'=4,'core'=2,'zl'=4,'x'=4] {'y'}, dimensions={0} | all-to-all | bytes 3145728 | tf_op jit(solution)/shard_map/all_to_all | solution.py:40
  57.0 7.3 %collective-permute-start = (bf16[2048,384]{1,0:T(8,128)(2,1)S(1)}, bf16[2048,384]{1,0:T(8,128)(2,1)S(1)}, u32[]{:S(2)}, u32[]{:S(2)}) collective-permute-start(bf16[2048,384]{1,0:T(8,128)(2,1)S(1)} %bitcast.14), channel_id=1, source_target_pairs={{0,16},{16,0},{1,17},{17,1},{2,18},{18,2},{3,19},{19,3},{4,20},{20... | collective-permute-start | bytes 4718600 | tf_op jit(solution)/shard_map/ppermute | solution.py:48
  64.5 1.6 copy-done
  66.1 2.9 %shard_map.110 = (bf16[256,2048]{1,0:T(8,128)(2,1)S(1)}, bf16[256,2048]{1,0:T(8,128)(2,1)S(1)}, bf16[2048,256]{1,0:T(8,128)(2,1)S(1)}, bf16[2048,256]{1,0:T(8,128)(2,1)}) custom-call(s32[4]{0:T(128)S(1)} %pad_add_fusion.ids.refs_0_, bf16[256,4096]{1,0:T(8,128)(2,1)S(1)} %copy-done), custom_call_target="tpu_custom_call" | custom-call | bytes 6291456 | tf_op jit(solution)/shard_map/pallas_call | solution.py:88
  70.0 1.5 shard_map.111
  72.1 19.5 %all-gather.1 = bf16[1024,128]{1,0:T(8,128)(2,1)S(1)} all-gather(bf16[128,128]{1,0:T(8,128)(2,1)S(1)} %get-tuple-element.29), channel_id=3, replica_groups=mesh['y'=4,'zh'=4,'core'=2,'zl'=4,'x'=4] {'zh','core'}, dimensions={0}, use_global_device_ids=true | all-gather | bytes 294912 | tf_op jit(solution)/shard_map/all_gather | solution.py:378
  92.9 3.3 %all-to-all-start.1 = ((bf16[4,128,128]{2,1,0:T(8,128)(2,1)}), bf16[4,128,128]{2,1,0:T(8,128)(2,1)S(1)}, u32[]{:S(2)}, u32[]{:S(2)}) async-start(bf16[4,128,128]{2,1,0:T(8,128)(2,1)} %shard_map.113), calls=%async_computation.1 | async-start | bytes 262144 | tf_op jit(solution)/shard_map/all_to_all | solution.py:44
  96.3 1.8 shard_map.116
  98.2 3.1 %collective-permute-start.1 = (bf16[512,384]{1,0:T(8,128)(2,1)}, bf16[512,384]{1,0:T(8,128)(2,1)S(1)}, u32[]{:S(2)}, u32[]{:S(2)}) collective-permute-start(bf16[512,384]{1,0:T(8,128)(2,1)} %get-tuple-element.34), channel_id=1, source_target_pairs={{0,1},{1,2},{2,3},{3,0},{4,5},{5,6},{6,7},{7,4},{8,9},{9,10},{10,1... | collective-permute-start | bytes 1179656 | tf_op jit(solution)/shard_map/ppermute | solution.py:52
  101.3 4.4 %collective-permute-start.2 = (bf16[512,384]{1,0:T(8,128)(2,1)}, bf16[512,384]{1,0:T(8,128)(2,1)S(1)}, u32[]{:S(2)}, u32[]{:S(2)}) collective-permute-start(bf16[512,384]{1,0:T(8,128)(2,1)} %get-tuple-element.35), channel_id=1, source_target_pairs={{0,2},{1,3},{2,0},{3,1},{4,6},{5,7},{6,4},{7,5},{8,10},{9,11},{10,... | collective-permute-start | bytes 1179656 | tf_op jit(solution)/shard_map/ppermute | solution.py:52
  105.7 3.1 %collective-permute-start.3 = (bf16[512,384]{1,0:T(8,128)(2,1)}, bf16[512,384]{1,0:T(8,128)(2,1)S(1)}, u32[]{:S(2)}, u32[]{:S(2)}) collective-permute-start(bf16[512,384]{1,0:T(8,128)(2,1)} %get-tuple-element.36), channel_id=1, source_target_pairs={{0,3},{1,0},{2,1},{3,2},{4,7},{5,4},{6,5},{7,6},{8,11},{9,8},{10,9... | collective-permute-start | bytes 1179656 | tf_op jit(solution)/shard_map/ppermute | solution.py:52
  111.4 1.9 shard_map.114
  113.4 19.4 %all-gather.3 = bf16[1024,128]{1,0:T(8,128)(2,1)S(1)} all-gather(bf16[128,128]{1,0:T(8,128)(2,1)S(1)} %get-tuple-element.32), channel_id=5, replica_groups=mesh['y'=4,'zh'=4,'core'=2,'zl'=4,'x'=4] {'zh','core'}, dimensions={0}, use_global_device_ids=true | all-gather | bytes 294912 | tf_op jit(solution)/shard_map/all_gather | solution.py:386
  135.0 2.1 collective-permute-start.4
  137.1 2.3 collective-permute-start.5
  139.3 4.6 %all-to-all-start.2 = ((bf16[16,128,128]{2,1,0:T(8,128)(2,1)}), bf16[16,128,128]{2,1,0:T(8,128)(2,1)S(1)}, u32[]{:S(2)}, u32[]{:S(2)}) async-start(bf16[16,128,128]{2,1,0:T(8,128)(2,1)} %bitcast.9.after), calls=%async_computation.2 | async-start | bytes 1048576 | tf_op jit(solution)/shard_map/all_to_all | solution.py:44
  143.9 10.9 %all-to-all-done.2 = bf16[16,128,128]{2,1,0:T(8,128)(2,1)S(1)} async-done(((bf16[16,128,128]{2,1,0:T(8,128)(2,1)}), bf16[16,128,128]{2,1,0:T(8,128)(2,1)S(1)}, u32[]{:S(2)}, u32[]{:S(2)}) %all-to-all-start.2) | async-done | bytes 524320 | tf_op jit(solution)/shard_map/all_to_all | solution.py:44
  156.1 3.5 %collective-permute-start.6 = (bf16[256,384]{1,0:T(8,128)(2,1)S(1)}, bf16[256,384]{1,0:T(8,128)(2,1)S(1)}, u32[]{:S(2)}, u32[]{:S(2)}) collective-permute-start(bf16[256,384]{1,0:T(8,128)(2,1)S(1)} %shard_map.118.parts), channel_id=1, source_target_pairs={{0,16},{16,0},{1,17},{17,1},{2,18},{18,2},{3,19},{19,3},{4,20},{20... | collective-permute-start | bytes 589832 | tf_op jit(solution)/shard_map/ppermute | solution.py:48
  160.7 2.4 shard_map.119.after
  164.4 4.3 %shard_map.120 = bf16[256,1024]{1,0:T(8,128)(2,1)} custom-call(s32[4]{0:T(128)S(1)} %pad_add_fusion.ids.refs_0_, bf16[4,256,640]{2,1,0:T(8,128)(2,1)S(1)} %bitcast.21, bf16[4,4,128,128]{3,2,1,0:T(8,128)(2,1)S(1)} %bitcast.18, bf16[4,512,384]{2,1,0:T(8,128)(2,1)S(1)} %shard_map.117.own, bf16[4,512,384]{2,1,0:T(8,128)(2,1)} %collective-permute-done.4.other, ...), custom_call_target="tpu_custom_call" | custom-call | flops 805306368 | bytes 5242880 | tf_op jit(solution)/shard_map/pallas_call | solution.py:289
  168.7 3.5 %all-to-all-start.3 = ((bf16[4,64,1024]{2,1,0:T(8,128)(2,1)}), bf16[4,64,1024]{2,1,0:T(8,128)(2,1)S(1)}, u32[]{:S(2)}, u32[]{:S(2)}) async-start(bf16[4,64,1024]{2,1,0:T(8,128)(2,1)} %bitcast.12), calls=%async_computation.3 | async-start | bytes 1048576 | tf_op jit(solution)/shard_map/all_to_all | solution.py:44
  172.8 13.6 %all-to-all-done.3.pieces = bf16[4,64,1024]{2,1,0:T(8,128)(2,1)S(1)} async-done(((bf16[4,64,1024]{2,1,0:T(8,128)(2,1)}), bf16[4,64,1024]{2,1,0:T(8,128)(2,1)S(1)}, u32[]{:S(2)}, u32[]{:S(2)}) %all-to-all-start.3) | async-done | bytes 524320 | tf_op jit(solution)/shard_map/all_to_all | solution.py:44
  186.5 16.0 %all_to_all.31 = bf16[4,64,1024]{2,1,0:T(8,128)(2,1)S(1)} all-to-all(bf16[4,64,1024]{2,1,0:T(8,128)(2,1)S(1)} %shard_map.121), channel_id=1, replica_groups=mesh['y'=4,'zh'=4,'core'=2,'zl'=4,'x'=4] {'zl'}, dimensions={0} | all-to-all | bytes 1048576 | tf_op jit(solution)/shard_map/all_to_all | solution.py:44
  202.4 1.6 broadcast_in_dim.15
  204.0 3.6 %all-to-all-start.5 = ((bf16[4,256,1024]{2,1,0:T(8,128)(2,1)}), bf16[4,256,1024]{2,1,0:T(8,128)(2,1)S(1)}, u32[]{:S(2)}, u32[]{:S(2)}) async-start(bf16[4,256,1024]{2,1,0:T(8,128)(2,1)} %broadcast_in_dim.15), calls=%async_computation.5 | async-start | bytes 4194304 | tf_op jit(solution)/shard_map/all_to_all | solution.py:40
  209.3 3.5 %collective-permute-start.7 = (bf16[128,384]{1,0:T(8,128)(2,1)S(1)}, bf16[128,384]{1,0:T(8,128)(2,1)S(1)}, u32[]{:S(2)}, u32[]{:S(2)}) collective-permute-start(bf16[128,384]{1,0:T(8,128)(2,1)S(1)} %get-tuple-element.40), channel_id=1, source_target_pairs={{0,32},{32,64},{64,96},{96,0},{1,33},{33,65},{65,97},{97,1},{2,34}... | collective-permute-start | bytes 294920 | tf_op jit(solution)/shard_map/ppermute | solution.py:52
  212.8 7.0 %collective-permute-start.8 = (bf16[128,384]{1,0:T(8,128)(2,1)S(1)}, bf16[128,384]{1,0:T(8,128)(2,1)S(1)}, u32[]{:S(2)}, u32[]{:S(2)}) collective-permute-start(bf16[128,384]{1,0:T(8,128)(2,1)S(1)} %get-tuple-element.41), channel_id=1, source_target_pairs={{0,64},{32,96},{64,0},{96,32},{1,65},{33,97},{65,1},{97,33},{2,66}... | collective-permute-start | bytes 294920 | tf_op jit(solution)/shard_map/ppermute | solution.py:52
  219.8 6.0 %collective-permute-start.9 = (bf16[128,384]{1,0:T(8,128)(2,1)S(1)}, bf16[128,384]{1,0:T(8,128)(2,1)S(1)}, u32[]{:S(2)}, u32[]{:S(2)}) collective-permute-start(bf16[128,384]{1,0:T(8,128)(2,1)S(1)} %get-tuple-element.42), channel_id=1, source_target_pairs={{0,96},{32,0},{64,32},{96,64},{1,97},{33,1},{65,33},{97,65},{2,98}... | collective-permute-start | bytes 294920 | tf_op jit(solution)/shard_map/ppermute | solution.py:52
  225.8 6.3 %collective-permute-done.8 = bf16[128,384]{1,0:T(8,128)(2,1)S(1)} collective-permute-done((bf16[128,384]{1,0:T(8,128)(2,1)S(1)}, bf16[128,384]{1,0:T(8,128)(2,1)S(1)}, u32[]{:S(2)}, u32[]{:S(2)}) %collective-permute-start.8) | collective-permute-done | bytes 98336 | tf_op jit(solution)/shard_map/ppermute | solution.py:52
  232.1 8.1 %collective-permute-done.9 = bf16[128,384]{1,0:T(8,128)(2,1)S(1)} collective-permute-done((bf16[128,384]{1,0:T(8,128)(2,1)S(1)}, bf16[128,384]{1,0:T(8,128)(2,1)S(1)}, u32[]{:S(2)}, u32[]{:S(2)}) %collective-permute-start.9) | collective-permute-done | bytes 98336 | tf_op jit(solution)/shard_map/ppermute | solution.py:52
  240.9 1.8 shard_map.122
  (49 shorter events, 15.5 us)
Async XLA Ops:
  57.0 12.9 %collective-permute-start = (bf16[2048,384]{1,0:T(8,128)(2,1)S(1)}, bf16[2048,384]{1,0:T(8,128)(2,1)S(1)}, u32[]{:S(2)}, u32[]{:S(2)}) collective-permute-start(bf16[2048,384]{1,0:T(8,128)(2,1)S(1)} %bitcast.14), channel_id=1, source_target_pairs={{0,16},{16,0},{1,17},{17,1},{2,18},{18,2},{3,19},{19,3},{4,20},{20... | collective-permute-start | bytes 4718600 | tf_op jit(solution)/shard_map/ppermute | solution.py:48
  64.5 1.6 copy-start
  69.0 1.0 copy-start.2
  70.0 21.7 %copy-start.8 = (f32[1,128,128]{2,1,0:T(8,128)S(1)}, f32[1,128,128]{2,1,0:T(8,128)}, u32[]{:S(2)}) copy-start(f32[1,128,128]{2,1,0:T(8,128)} %refs_2_.1) | copy-start | bytes 196612
  71.5 0.7 copy-start.5
  72.1 36.6 %copy-start.9 = (s32[2,2]{1,0:T(2,128)S(1)}, s32[2,2]{1,0:T(2,128)}, u32[]{:S(2)}) copy-start(s32[2,2]{1,0:T(2,128)} %mask.3) | copy-start | bytes 52
  92.9 16.7 %all-to-all-start.1 = ((bf16[4,128,128]{2,1,0:T(8,128)(2,1)}), bf16[4,128,128]{2,1,0:T(8,128)(2,1)S(1)}, u32[]{:S(2)}, u32[]{:S(2)}) async-start(bf16[4,128,128]{2,1,0:T(8,128)(2,1)} %shard_map.113), calls=%async_computation.1 | async-start | bytes 262144 | tf_op jit(solution)/shard_map/all_to_all | solution.py:44
  96.3 66.8 %all-gather.6.cloned.1.call-start = ((), (), s32[]{:S(2)}) async-start(), calls=%async_computation.8 | async-start | bytes 1638400 | tf_op jit(solution)/shard_map/all_gather | solution.py:385
  96.3 12.4 %copy-start.6 = (bf16[256,384]{1,0:T(8,128)(2,1)S(1)}, bf16[256,384]{1,0:T(8,128)(2,1)}, u32[]{:S(2)}) copy-start(bf16[256,384]{1,0:T(8,128)(2,1)} %copy-done.5) | copy-start | bytes 589828
  98.2 36.0 %collective-permute-start.1 = (bf16[512,384]{1,0:T(8,128)(2,1)}, bf16[512,384]{1,0:T(8,128)(2,1)S(1)}, u32[]{:S(2)}, u32[]{:S(2)}) collective-permute-start(bf16[512,384]{1,0:T(8,128)(2,1)} %get-tuple-element.34), channel_id=1, source_target_pairs={{0,1},{1,2},{2,3},{3,0},{4,5},{5,6},{6,7},{7,4},{8,9},{9,10},{10,1... | collective-permute-start | bytes 1179656 | tf_op jit(solution)/shard_map/ppermute | solution.py:52
  101.3 32.9 %collective-permute-start.2 = (bf16[512,384]{1,0:T(8,128)(2,1)}, bf16[512,384]{1,0:T(8,128)(2,1)S(1)}, u32[]{:S(2)}, u32[]{:S(2)}) collective-permute-start(bf16[512,384]{1,0:T(8,128)(2,1)} %get-tuple-element.35), channel_id=1, source_target_pairs={{0,2},{1,3},{2,0},{3,1},{4,6},{5,7},{6,4},{7,5},{8,10},{9,11},{10,... | collective-permute-start | bytes 1179656 | tf_op jit(solution)/shard_map/ppermute | solution.py:52
  105.7 28.6 %collective-permute-start.3 = (bf16[512,384]{1,0:T(8,128)(2,1)}, bf16[512,384]{1,0:T(8,128)(2,1)S(1)}, u32[]{:S(2)}, u32[]{:S(2)}) collective-permute-start(bf16[512,384]{1,0:T(8,128)(2,1)} %get-tuple-element.36), channel_id=1, source_target_pairs={{0,3},{1,0},{2,1},{3,2},{4,7},{5,4},{6,5},{7,6},{8,11},{9,8},{10,9... | collective-permute-start | bytes 1179656 | tf_op jit(solution)/shard_map/ppermute | solution.py:52
  109.6 0.9 copy-start.7
  110.6 0.8 copy-start.10
  135.0 28.1 %collective-permute-start.4 = (bf16[4,512,384]{2,1,0:T(8,128)(2,1)S(1)}, bf16[4,512,384]{2,1,0:T(8,128)(2,1)}, u32[]{:S(2)}, u32[]{:S(2)}) collective-permute-start(bf16[4,512,384]{2,1,0:T(8,128)(2,1)S(1)} %shard_map.117.own), channel_id=1, source_target_pairs={{0,16},{16,0},{1,17},{17,1},{2,18},{18,2},{3,19},{19,3},{4,20},{20... | collective-permute-start | bytes 4718600 | tf_op jit(solution)/shard_map/ppermute | solution.py:48
  137.1 6.9 %collective-permute-start.5 = (bf16[2048,256]{1,0:T(8,128)(2,1)}, bf16[2048,256]{1,0:T(8,128)(2,1)S(1)}, u32[]{:S(2)}, u32[]{:S(2)}) collective-permute-start(bf16[2048,256]{1,0:T(8,128)(2,1)} %get-tuple-element.38), channel_id=1, source_target_pairs={{0,16},{16,0},{1,17},{17,1},{2,18},{18,2},{3,19},{19,3},{4,20},{20... | collective-permute-start | bytes 3145736 | tf_op jit(solution)/shard_map/ppermute | solution.py:48
  139.3 15.5 %all-to-all-start.2 = ((bf16[16,128,128]{2,1,0:T(8,128)(2,1)}), bf16[16,128,128]{2,1,0:T(8,128)(2,1)S(1)}, u32[]{:S(2)}, u32[]{:S(2)}) async-start(bf16[16,128,128]{2,1,0:T(8,128)(2,1)} %bitcast.9.after), calls=%async_computation.2 | async-start | bytes 1048576 | tf_op jit(solution)/shard_map/all_to_all | solution.py:44
  154.8 5.8 %copy-start.3 = (bf16[2048,256]{1,0:T(8,128)(2,1)S(1)}, bf16[2048,256]{1,0:T(8,128)(2,1)}, u32[]{:S(2)}) copy-start(bf16[2048,256]{1,0:T(8,128)(2,1)} %copy-done.2) | copy-start | bytes 3145732
  156.1 4.5 %collective-permute-start.6 = (bf16[256,384]{1,0:T(8,128)(2,1)S(1)}, bf16[256,384]{1,0:T(8,128)(2,1)S(1)}, u32[]{:S(2)}, u32[]{:S(2)}) collective-permute-start(bf16[256,384]{1,0:T(8,128)(2,1)S(1)} %shard_map.118.parts), channel_id=1, source_target_pairs={{0,16},{16,0},{1,17},{17,1},{2,18},{18,2},{3,19},{19,3},{4,20},{20... | collective-permute-start | bytes 589832 | tf_op jit(solution)/shard_map/ppermute | solution.py:48
  163.1 1.3 copy-start.1
  168.7 17.7 %all-to-all-start.3 = ((bf16[4,64,1024]{2,1,0:T(8,128)(2,1)}), bf16[4,64,1024]{2,1,0:T(8,128)(2,1)S(1)}, u32[]{:S(2)}, u32[]{:S(2)}) async-start(bf16[4,64,1024]{2,1,0:T(8,128)(2,1)} %bitcast.12), calls=%async_computation.3 | async-start | bytes 1048576 | tf_op jit(solution)/shard_map/all_to_all | solution.py:44
  172.2 35.5 %reduce-scatter.2.cloned.1.call-start = ((), (), s32[]{:S(2)}) async-start(), calls=%async_computation.7 | async-start | bytes 1966080 | tf_op jit(solution)/shard_map/reduce_scatter | solution.py:399
  204.0 36.8 %all-to-all-start.5 = ((bf16[4,256,1024]{2,1,0:T(8,128)(2,1)}), bf16[4,256,1024]{2,1,0:T(8,128)(2,1)S(1)}, u32[]{:S(2)}, u32[]{:S(2)}) async-start(bf16[4,256,1024]{2,1,0:T(8,128)(2,1)} %broadcast_in_dim.15), calls=%async_computation.5 | async-start | bytes 4194304 | tf_op jit(solution)/shard_map/all_to_all | solution.py:40
  207.7 1.0 copy-start.4
  209.3 16.5 %collective-permute-start.7 = (bf16[128,384]{1,0:T(8,128)(2,1)S(1)}, bf16[128,384]{1,0:T(8,128)(2,1)S(1)}, u32[]{:S(2)}, u32[]{:S(2)}) collective-permute-start(bf16[128,384]{1,0:T(8,128)(2,1)S(1)} %get-tuple-element.40), channel_id=1, source_target_pairs={{0,32},{32,64},{64,96},{96,0},{1,33},{33,65},{65,97},{97,1},{2,34}... | collective-permute-start | bytes 294920 | tf_op jit(solution)/shard_map/ppermute | solution.py:52
  212.8 19.3 %collective-permute-start.8 = (bf16[128,384]{1,0:T(8,128)(2,1)S(1)}, bf16[128,384]{1,0:T(8,128)(2,1)S(1)}, u32[]{:S(2)}, u32[]{:S(2)}) collective-permute-start(bf16[128,384]{1,0:T(8,128)(2,1)S(1)} %get-tuple-element.41), channel_id=1, source_target_pairs={{0,64},{32,96},{64,0},{96,32},{1,65},{33,97},{65,1},{97,33},{2,66}... | collective-permute-start | bytes 294920 | tf_op jit(solution)/shard_map/ppermute | solution.py:52
  219.8 20.4 %collective-permute-start.9 = (bf16[128,384]{1,0:T(8,128)(2,1)S(1)}, bf16[128,384]{1,0:T(8,128)(2,1)S(1)}, u32[]{:S(2)}, u32[]{:S(2)}) collective-permute-start(bf16[128,384]{1,0:T(8,128)(2,1)S(1)} %get-tuple-element.42), channel_id=1, source_target_pairs={{0,96},{32,0},{64,32},{96,64},{1,97},{33,1},{65,33},{97,65},{2,98}... | collective-permute-start | bytes 294920 | tf_op jit(solution)/shard_map/ppermute | solution.py:52
Sparse Core Ops, SparseCore 0:
  113.5 25.5 all-gather.5
Sparse Core Ops, SparseCore 1:
  175.5 24.6 reduce-scatter.1

commit v4 on v3

--- a/solution.py
+++ b/solution.py
@@ -392,7 +392,7 @@
     parts = own_parts(ids, early, states, crossed)
 
     grads = weight_terms(own_turned, crossed, parts, swap(parts))
-    term = back_terms(ids, heads, states, back_own, back_other, grads)
+    term = back_terms(ids, heads, states, back_own, back_other, parts)
     summed = summed_for_all(trade(term.reshape(4, 64, 1024), "zl"))
     gathered = trade(summed, "zl").reshape(256, 1024)
     events_grad = lay_out(spread(gathered, "x"))

time: 251 us -> 244 us (0.972)
  waiting for transfers between devices: 40.5 us -> 33.5 us
    all_to_all x3, waiting for transfers between devices: 24.5 us -> 17.8 us  [trade(): return lax.all_to_all(pieces, axis, 0, 0)]
where the time goes in v4:
time: 244 us; the launch traced here: 243 us
  blocking collectives  103 us (42%)
  starting transfers between devices  58.9 us (24%)
  waiting for transfers between devices  33.5 us (14%)
  Pallas kernels  22 us (9%)
  between operations  15.8 us (6%)
  local copies, waits for them, and re-layouts  8.79 us (4%)
    ppermute x6, starting transfers between devices, shift(): return lax.ppermute(piece, axis, [(i, (i + k) % 4) for i in range(4)])  28.6 us
    all_gather x1, blocking collectives, on_device(): own = spread(lax.all_gather(shard, 'zh'), 'y').reshape(2048, 384)  27.8 us
    all_to_all x1, blocking collectives, spread(): lax.all_to_all(jnp.broadcast_to(array[None], (count, *array.shape)), axis...  20.2 us
    all_gather x1, blocking collectives, on_device(): near = lax.all_gather(local_state, ('zh', 'core'))  19.5 us
    all_gather x1, blocking collectives, on_device(): near = lax.all_gather(local_grad, ('zh', 'core'))  19.4 us
    all_to_all x3, waiting for transfers between devices, trade(): return lax.all_to_all(pieces, axis, 0, 0)  17.8 us
    all_to_all x1, blocking collectives, trade(): return lax.all_to_all(pieces, axis, 0, 0)  16.2 us
    ppermute x4, starting transfers between devices, swap(): return lax.ppermute(array, 'core', ((0, 1), (1, 0)))  15.1 us
  transfers between devices with their start and end apart: 16, of which 5 were waited for; matrix products, arithmetic and copies ran while one was open for 1% of the time, Pallas kernels for 6%

profile of v4, /device:TPU:1, one launch (start us, length us, event | category | flops | bytes accessed | tf_op | source)
XLA Modules:
  0.0 243.1 jit_solution(18341340918824983401)
XLA Ops:
  8.8 27.8 %all-gather = bf16[512,384]{1,0:T(8,128)(2,1)S(1)} all-gather(bf16[128,384]{1,0:T(8,128)(2,1)S(1)} %pad_maximum_fusion), channel_id=2, replica_groups=mesh['y'=4,'zh'=4,'core'=2,'zl'=4,'x'=4] {'zh'}, dimensions={0}, use_global_device_ids=true | all-gather | bytes 491520 | tf_op jit(solution)/shard_map/all_gather | solution.py:374
  36.8 20.2 %all_to_all.30 = bf16[4,4,128,384]{3,2,1,0:T(8,128)(2,1)S(1)} all-to-all(bf16[4,4,128,384]{3,2,1,0:T(8,128)(2,1)S(1)} %broadcast_in_dim.6), channel_id=1, replica_groups=mesh['y'=4,'zh'=4,'core'=2,'zl'=4,'x'=4] {'y'}, dimensions={0} | all-to-all | bytes 3145728 | tf_op jit(solution)/shard_map/all_to_all | solution.py:40
  57.0 7.3 %collective-permute-start = (bf16[2048,384]{1,0:T(8,128)(2,1)S(1)}, bf16[2048,384]{1,0:T(8,128)(2,1)S(1)}, u32[]{:S(2)}, u32[]{:S(2)}) collective-permute-start(bf16[2048,384]{1,0:T(8,128)(2,1)S(1)} %bitcast.14), channel_id=1, source_target_pairs={{0,16},{16,0},{1,17},{17,1},{2,18},{18,2},{3,19},{19,3},{4,20},{20... | collective-permute-start | bytes 4718600 | tf_op jit(solution)/shard_map/ppermute | solution.py:48
  64.5 1.6 copy-done.1
  66.1 2.9 %shard_map.110 = (bf16[256,2048]{1,0:T(8,128)(2,1)S(1)}, bf16[256,2048]{1,0:T(8,128)(2,1)S(1)}, bf16[2048,256]{1,0:T(8,128)(2,1)S(1)}, bf16[2048,256]{1,0:T(8,128)(2,1)}) custom-call(s32[4]{0:T(128)S(1)} %pad_add_fusion.ids.refs_0_, bf16[256,4096]{1,0:T(8,128)(2,1)S(1)} %copy-done.1), custom_call_target="tpu_custom_call" | custom-call | bytes 6291456 | tf_op jit(solution)/shard_map/pallas_call | solution.py:88
  70.0 1.5 shard_map.111
  72.1 19.5 %all-gather.1 = bf16[1024,128]{1,0:T(8,128)(2,1)S(1)} all-gather(bf16[128,128]{1,0:T(8,128)(2,1)S(1)} %get-tuple-element.29), channel_id=3, replica_groups=mesh['y'=4,'zh'=4,'core'=2,'zl'=4,'x'=4] {'zh','core'}, dimensions={0}, use_global_device_ids=true | all-gather | bytes 294912 | tf_op jit(solution)/shard_map/all_gather | solution.py:378
  92.9 3.3 %all-to-all-start.1 = ((bf16[4,128,128]{2,1,0:T(8,128)(2,1)}), bf16[4,128,128]{2,1,0:T(8,128)(2,1)S(1)}, u32[]{:S(2)}, u32[]{:S(2)}) async-start(bf16[4,128,128]{2,1,0:T(8,128)(2,1)} %shard_map.113), calls=%async_computation.1 | async-start | bytes 262144 | tf_op jit(solution)/shard_map/all_to_all | solution.py:44
  96.3 1.7 shard_map.116
  98.0 3.1 %collective-permute-start.1 = (bf16[512,384]{1,0:T(8,128)(2,1)}, bf16[512,384]{1,0:T(8,128)(2,1)S(1)}, u32[]{:S(2)}, u32[]{:S(2)}) collective-permute-start(bf16[512,384]{1,0:T(8,128)(2,1)} %get-tuple-element.34), channel_id=1, source_target_pairs={{0,1},{1,2},{2,3},{3,0},{4,5},{5,6},{6,7},{7,4},{8,9},{9,10},{10,1... | collective-permute-start | bytes 1179656 | tf_op jit(solution)/shard_map/ppermute | solution.py:52
  101.1 4.4 %collective-permute-start.2 = (bf16[512,384]{1,0:T(8,128)(2,1)}, bf16[512,384]{1,0:T(8,128)(2,1)S(1)}, u32[]{:S(2)}, u32[]{:S(2)}) collective-permute-start(bf16[512,384]{1,0:T(8,128)(2,1)} %get-tuple-element.35), channel_id=1, source_target_pairs={{0,2},{1,3},{2,0},{3,1},{4,6},{5,7},{6,4},{7,5},{8,10},{9,11},{10,... | collective-permute-start | bytes 1179656 | tf_op jit(solution)/shard_map/ppermute | solution.py:52
  105.5 3.1 %collective-permute-start.3 = (bf16[512,384]{1,0:T(8,128)(2,1)S(1)}, bf16[512,384]{1,0:T(8,128)(2,1)S(1)}, u32[]{:S(2)}, u32[]{:S(2)}) collective-permute-start(bf16[512,384]{1,0:T(8,128)(2,1)S(1)} %get-tuple-element.36), channel_id=1, source_target_pairs={{0,3},{1,0},{2,1},{3,2},{4,7},{5,4},{6,5},{7,6},{8,11},{9,8},{10,9... | collective-permute-start | bytes 1179656 | tf_op jit(solution)/shard_map/ppermute | solution.py:52
  109.5 1.9 shard_map.114
  111.4 19.4 %all-gather.3 = bf16[1024,128]{1,0:T(8,128)(2,1)S(1)} all-gather(bf16[128,128]{1,0:T(8,128)(2,1)S(1)} %get-tuple-element.32), channel_id=5, replica_groups=mesh['y'=4,'zh'=4,'core'=2,'zl'=4,'x'=4] {'zh','core'}, dimensions={0}, use_global_device_ids=true | all-gather | bytes 294912 | tf_op jit(solution)/shard_map/all_gather | solution.py:386
  133.1 2.1 collective-permute-start.4
  135.2 2.3 collective-permute-start.5
  137.4 4.6 %all-to-all-start.2 = ((bf16[16,128,128]{2,1,0:T(8,128)(2,1)}), bf16[16,128,128]{2,1,0:T(8,128)(2,1)S(1)}, u32[]{:S(2)}, u32[]{:S(2)}) async-start(bf16[16,128,128]{2,1,0:T(8,128)(2,1)} %bitcast.9.after), calls=%async_computation.2 | async-start | bytes 1048576 | tf_op jit(solution)/shard_map/all_to_all | solution.py:44
  142.0 10.9 %all-to-all-done.2 = bf16[16,128,128]{2,1,0:T(8,128)(2,1)S(1)} async-done(((bf16[16,128,128]{2,1,0:T(8,128)(2,1)}), bf16[16,128,128]{2,1,0:T(8,128)(2,1)S(1)}, u32[]{:S(2)}, u32[]{:S(2)}) %all-to-all-start.2) | async-done | bytes 524320 | tf_op jit(solution)/shard_map/all_to_all | solution.py:44
  155.5 3.5 %shard_map.119 = bf16[256,1024]{1,0:T(8,128)(2,1)S(1)} custom-call(s32[4]{0:T(128)S(1)} %pad_add_fusion.ids.refs_0_, bf16[4,256,640]{2,1,0:T(8,128)(2,1)S(1)} %bitcast.22, bf16[4,4,128,128]{3,2,1,0:T(8,128)(2,1)S(1)} %bitcast.18, bf16[4,512,384]{2,1,0:T(8,128)(2,1)S(1)} %shard_map.117.own, bf16[4,512,384]{2,1,0:T(8,128)(2,1)} %collective-permute-done.4.other, ...), custom_call_target="tpu_custom_call" | custom-call | flops 805306368 | bytes 5242880 | tf_op jit(solution)/shard_map/pallas_call | solution.py:289
  159.8 3.6 %all-to-all-start.3 = ((bf16[4,64,1024]{2,1,0:T(8,128)(2,1)}), bf16[4,64,1024]{2,1,0:T(8,128)(2,1)S(1)}, u32[]{:S(2)}, u32[]{:S(2)}) async-start(bf16[4,64,1024]{2,1,0:T(8,128)(2,1)} %bitcast.21), calls=%async_computation.3 | async-start | bytes 1048576 | tf_op jit(solution)/shard_map/all_to_all | solution.py:44
  163.4 3.5 %collective-permute-start.6 = (bf16[256,384]{1,0:T(8,128)(2,1)S(1)}, bf16[256,384]{1,0:T(8,128)(2,1)S(1)}, u32[]{:S(2)}, u32[]{:S(2)}) collective-permute-start(bf16[256,384]{1,0:T(8,128)(2,1)S(1)} %shard_map.118.after.parts), channel_id=1, source_target_pairs={{0,16},{16,0},{1,17},{17,1},{2,18},{18,2},{3,19},{19,3},{4,20},{20... | collective-permute-start | bytes 589832 | tf_op jit(solution)/shard_map/ppermute | solution.py:48
  168.0 2.5 %shard_map.122 = bf16[2048,384]{1,0:T(8,128)(2,1)} custom-call(bf16[2048,256]{1,0:T(8,128)(2,1)S(1)} %copy-done.4, bf16[2048,256]{1,0:T(8,128)(2,1)S(1)} %collective-permute-done.5.after.crossed, bf16[256,384]{1,0:T(8,128)(2,1)S(1)} %shard_map.118.after.parts, bf16[256,384]{1,0:T(8,128)(2,1)S(1)} %collective-permute-done.6.other), custom_call_target="tpu_custom_call" | custom-call | flops 805306368 | bytes 5242880 | tf_op jit(solution)/shard_map/pallas_call | solution.py:314
  170.5 6.9 %all-to-all-done.3.pieces = bf16[4,64,1024]{2,1,0:T(8,128)(2,1)S(1)} async-done(((bf16[4,64,1024]{2,1,0:T(8,128)(2,1)}), bf16[4,64,1024]{2,1,0:T(8,128)(2,1)S(1)}, u32[]{:S(2)}, u32[]{:S(2)}) %all-to-all-start.3) | async-done | bytes 524320 | tf_op jit(solution)/shard_map/all_to_all | solution.py:44
  177.4 16.2 %all_to_all.31 = bf16[4,64,1024]{2,1,0:T(8,128)(2,1)S(1)} all-to-all(bf16[4,64,1024]{2,1,0:T(8,128)(2,1)S(1)} %shard_map.120), channel_id=1, replica_groups=mesh['y'=4,'zh'=4,'core'=2,'zl'=4,'x'=4] {'zl'}, dimensions={0} | all-to-all | bytes 1048576 | tf_op jit(solution)/shard_map/all_to_all | solution.py:44
  193.6 1.6 broadcast_in_dim.15
  195.3 3.6 %all-to-all-start.5 = ((bf16[4,256,1024]{2,1,0:T(8,128)(2,1)}), bf16[4,256,1024]{2,1,0:T(8,128)(2,1)S(1)}, u32[]{:S(2)}, u32[]{:S(2)}) async-start(bf16[4,256,1024]{2,1,0:T(8,128)(2,1)} %broadcast_in_dim.15), calls=%async_computation.5 | async-start | bytes 4194304 | tf_op jit(solution)/shard_map/all_to_all | solution.py:40
  200.5 3.7 %collective-permute-start.7 = (bf16[128,384]{1,0:T(8,128)(2,1)S(1)}, bf16[128,384]{1,0:T(8,128)(2,1)S(1)}, u32[]{:S(2)}, u32[]{:S(2)}) collective-permute-start(bf16[128,384]{1,0:T(8,128)(2,1)S(1)} %get-tuple-element.40), channel_id=1, source_target_pairs={{0,32},{32,64},{64,96},{96,0},{1,33},{33,65},{65,97},{97,1},{2,34}... | collective-permute-start | bytes 294920 | tf_op jit(solution)/shard_map/ppermute | solution.py:52
  204.2 7.7 %collective-permute-start.8 = (bf16[128,384]{1,0:T(8,128)(2,1)S(1)}, bf16[128,384]{1,0:T(8,128)(2,1)S(1)}, u32[]{:S(2)}, u32[]{:S(2)}) collective-permute-start(bf16[128,384]{1,0:T(8,128)(2,1)S(1)} %get-tuple-element.41), channel_id=1, source_target_pairs={{0,64},{32,96},{64,0},{96,32},{1,65},{33,97},{65,1},{97,33},{2,66}... | collective-permute-start | bytes 294920 | tf_op jit(solution)/shard_map/ppermute | solution.py:52
  211.9 6.6 %collective-permute-start.9 = (bf16[128,384]{1,0:T(8,128)(2,1)S(1)}, bf16[128,384]{1,0:T(8,128)(2,1)S(1)}, u32[]{:S(2)}, u32[]{:S(2)}) collective-permute-start(bf16[128,384]{1,0:T(8,128)(2,1)S(1)} %get-tuple-element.42), channel_id=1, source_target_pairs={{0,96},{32,0},{64,32},{96,64},{1,97},{33,1},{65,33},{97,65},{2,98}... | collective-permute-start | bytes 294920 | tf_op jit(solution)/shard_map/ppermute | solution.py:52
  218.5 6.3 %collective-permute-done.8 = bf16[128,384]{1,0:T(8,128)(2,1)S(1)} collective-permute-done((bf16[128,384]{1,0:T(8,128)(2,1)S(1)}, bf16[128,384]{1,0:T(8,128)(2,1)S(1)}, u32[]{:S(2)}, u32[]{:S(2)}) %collective-permute-start.8) | collective-permute-done | bytes 98336 | tf_op jit(solution)/shard_map/ppermute | solution.py:52
  224.9 8.3 %collective-permute-done.9 = bf16[128,384]{1,0:T(8,128)(2,1)S(1)} collective-permute-done((bf16[128,384]{1,0:T(8,128)(2,1)S(1)}, bf16[128,384]{1,0:T(8,128)(2,1)S(1)}, u32[]{:S(2)}, u32[]{:S(2)}) %collective-permute-start.9) | collective-permute-done | bytes 98336 | tf_op jit(solution)/shard_map/ppermute | solution.py:52
  233.9 1.8 shard_map.121
  (49 shorter events, 14.0 us)
Async XLA Ops:
  57.0 12.9 %collective-permute-start = (bf16[2048,384]{1,0:T(8,128)(2,1)S(1)}, bf16[2048,384]{1,0:T(8,128)(2,1)S(1)}, u32[]{:S(2)}, u32[]{:S(2)}) collective-permute-start(bf16[2048,384]{1,0:T(8,128)(2,1)S(1)} %bitcast.14), channel_id=1, source_target_pairs={{0,16},{16,0},{1,17},{17,1},{2,18},{18,2},{3,19},{19,3},{4,20},{20... | collective-permute-start | bytes 4718600 | tf_op jit(solution)/shard_map/ppermute | solution.py:48
  64.5 1.6 copy-start.1
  69.0 1.0 copy-start.3
  70.0 21.7 %copy-start.8 = (f32[1,128,128]{2,1,0:T(8,128)S(1)}, f32[1,128,128]{2,1,0:T(8,128)}, u32[]{:S(2)}) copy-start(f32[1,128,128]{2,1,0:T(8,128)} %refs_2_.1) | copy-start | bytes 196612
  71.4 0.7 copy-start.6
  72.1 36.4 %copy-start.9 = (s32[2,2]{1,0:T(2,128)S(1)}, s32[2,2]{1,0:T(2,128)}, u32[]{:S(2)}) copy-start(s32[2,2]{1,0:T(2,128)} %mask.3) | copy-start | bytes 52
  72.1 37.3 %copy-start.10 = (bf16[256,128]{1,0:T(8,128)(2,1)S(1)}, bf16[256,128]{1,0:T(8,128)(2,1)}, u32[]{:S(2)}) copy-start(bf16[256,128]{1,0:T(8,128)(2,1)} %cotangent.1) | copy-start | bytes 196612
  72.1 36.4 %copy-start.7 = (bf16[256,384]{1,0:T(8,128)(2,1)S(1)}, bf16[256,384]{1,0:T(8,128)(2,1)}, u32[]{:S(2)}) copy-start(bf16[256,384]{1,0:T(8,128)(2,1)} %copy-done.6) | copy-start | bytes 589828
  92.9 16.5 %all-to-all-start.1 = ((bf16[4,128,128]{2,1,0:T(8,128)(2,1)}), bf16[4,128,128]{2,1,0:T(8,128)(2,1)S(1)}, u32[]{:S(2)}, u32[]{:S(2)}) async-start(bf16[4,128,128]{2,1,0:T(8,128)(2,1)} %shard_map.113), calls=%async_computation.1 | async-start | bytes 262144 | tf_op jit(solution)/shard_map/all_to_all | solution.py:44
  96.3 57.9 %all-gather.6.cloned.1.call-start = ((), (), s32[]{:S(2)}) async-start(), calls=%async_computation.8 | async-start | bytes 1638400 | tf_op jit(solution)/shard_map/all_gather | solution.py:385
  98.0 34.3 %collective-permute-start.1 = (bf16[512,384]{1,0:T(8,128)(2,1)}, bf16[512,384]{1,0:T(8,128)(2,1)S(1)}, u32[]{:S(2)}, u32[]{:S(2)}) collective-permute-start(bf16[512,384]{1,0:T(8,128)(2,1)} %get-tuple-element.34), channel_id=1, source_target_pairs={{0,1},{1,2},{2,3},{3,0},{4,5},{5,6},{6,7},{7,4},{8,9},{9,10},{10,1... | collective-permute-start | bytes 1179656 | tf_op jit(solution)/shard_map/ppermute | solution.py:52
  101.1 31.2 %collective-permute-start.2 = (bf16[512,384]{1,0:T(8,128)(2,1)}, bf16[512,384]{1,0:T(8,128)(2,1)S(1)}, u32[]{:S(2)}, u32[]{:S(2)}) collective-permute-start(bf16[512,384]{1,0:T(8,128)(2,1)} %get-tuple-element.35), channel_id=1, source_target_pairs={{0,2},{1,3},{2,0},{3,1},{4,6},{5,7},{6,4},{7,5},{8,10},{9,11},{10,... | collective-permute-start | bytes 1179656 | tf_op jit(solution)/shard_map/ppermute | solution.py:52
  105.5 26.8 %collective-permute-start.3 = (bf16[512,384]{1,0:T(8,128)(2,1)S(1)}, bf16[512,384]{1,0:T(8,128)(2,1)S(1)}, u32[]{:S(2)}, u32[]{:S(2)}) collective-permute-start(bf16[512,384]{1,0:T(8,128)(2,1)S(1)} %get-tuple-element.36), channel_id=1, source_target_pairs={{0,3},{1,0},{2,1},{3,2},{4,7},{5,4},{6,5},{7,6},{8,11},{9,8},{10,9... | collective-permute-start | bytes 1179656 | tf_op jit(solution)/shard_map/ppermute | solution.py:52
  133.1 21.0 %collective-permute-start.4 = (bf16[4,512,384]{2,1,0:T(8,128)(2,1)S(1)}, bf16[4,512,384]{2,1,0:T(8,128)(2,1)}, u32[]{:S(2)}, u32[]{:S(2)}) collective-permute-start(bf16[4,512,384]{2,1,0:T(8,128)(2,1)S(1)} %shard_map.117.own), channel_id=1, source_target_pairs={{0,16},{16,0},{1,17},{17,1},{2,18},{18,2},{3,19},{19,3},{4,20},{20... | collective-permute-start | bytes 4718600 | tf_op jit(solution)/shard_map/ppermute | solution.py:48
  135.2 6.9 %collective-permute-start.5 = (bf16[2048,256]{1,0:T(8,128)(2,1)}, bf16[2048,256]{1,0:T(8,128)(2,1)S(1)}, u32[]{:S(2)}, u32[]{:S(2)}) collective-permute-start(bf16[2048,256]{1,0:T(8,128)(2,1)} %get-tuple-element.37), channel_id=1, source_target_pairs={{0,16},{16,0},{1,17},{17,1},{2,18},{18,2},{3,19},{19,3},{4,20},{20... | collective-permute-start | bytes 3145736 | tf_op jit(solution)/shard_map/ppermute | solution.py:48
  137.4 15.5 %all-to-all-start.2 = ((bf16[16,128,128]{2,1,0:T(8,128)(2,1)}), bf16[16,128,128]{2,1,0:T(8,128)(2,1)S(1)}, u32[]{:S(2)}, u32[]{:S(2)}) async-start(bf16[16,128,128]{2,1,0:T(8,128)(2,1)} %bitcast.9.after), calls=%async_computation.2 | async-start | bytes 1048576 | tf_op jit(solution)/shard_map/all_to_all | solution.py:44
  154.2 1.3 copy-start.2
  159.0 0.8 copy-start
  159.8 8.2 %copy-start.4 = (bf16[2048,256]{1,0:T(8,128)(2,1)S(1)}, bf16[2048,256]{1,0:T(8,128)(2,1)}, u32[]{:S(2)}) copy-start(bf16[2048,256]{1,0:T(8,128)(2,1)} %copy-done.3) | copy-start | bytes 3145732
  159.8 17.6 %all-to-all-start.3 = ((bf16[4,64,1024]{2,1,0:T(8,128)(2,1)}), bf16[4,64,1024]{2,1,0:T(8,128)(2,1)S(1)}, u32[]{:S(2)}, u32[]{:S(2)}) async-start(bf16[4,64,1024]{2,1,0:T(8,128)(2,1)} %bitcast.21), calls=%async_computation.3 | async-start | bytes 1048576 | tf_op jit(solution)/shard_map/all_to_all | solution.py:44
  163.4 35.5 %reduce-scatter.2.cloned.1.call-start = ((), (), s32[]{:S(2)}) async-start(), calls=%async_computation.7 | async-start | bytes 1966080 | tf_op jit(solution)/shard_map/reduce_scatter | solution.py:399
  163.4 4.5 %collective-permute-start.6 = (bf16[256,384]{1,0:T(8,128)(2,1)S(1)}, bf16[256,384]{1,0:T(8,128)(2,1)S(1)}, u32[]{:S(2)}, u32[]{:S(2)}) collective-permute-start(bf16[256,384]{1,0:T(8,128)(2,1)S(1)} %shard_map.118.after.parts), channel_id=1, source_target_pairs={{0,16},{16,0},{1,17},{17,1},{2,18},{18,2},{3,19},{19,3},{4,20},{20... | collective-permute-start | bytes 589832 | tf_op jit(solution)/shard_map/ppermute | solution.py:48
  195.3 38.6 %all-to-all-start.5 = ((bf16[4,256,1024]{2,1,0:T(8,128)(2,1)}), bf16[4,256,1024]{2,1,0:T(8,128)(2,1)S(1)}, u32[]{:S(2)}, u32[]{:S(2)}) async-start(bf16[4,256,1024]{2,1,0:T(8,128)(2,1)} %broadcast_in_dim.15), calls=%async_computation.5 | async-start | bytes 4194304 | tf_op jit(solution)/shard_map/all_to_all | solution.py:40
  198.9 1.0 copy-start.5
  200.5 18.0 %collective-permute-start.7 = (bf16[128,384]{1,0:T(8,128)(2,1)S(1)}, bf16[128,384]{1,0:T(8,128)(2,1)S(1)}, u32[]{:S(2)}, u32[]{:S(2)}) collective-permute-start(bf16[128,384]{1,0:T(8,128)(2,1)S(1)} %get-tuple-element.40), channel_id=1, source_target_pairs={{0,32},{32,64},{64,96},{96,0},{1,33},{33,65},{65,97},{97,1},{2,34}... | collective-permute-start | bytes 294920 | tf_op jit(solution)/shard_map/ppermute | solution.py:52
  204.2 20.7 %collective-permute-start.8 = (bf16[128,384]{1,0:T(8,128)(2,1)S(1)}, bf16[128,384]{1,0:T(8,128)(2,1)S(1)}, u32[]{:S(2)}, u32[]{:S(2)}) collective-permute-start(bf16[128,384]{1,0:T(8,128)(2,1)S(1)} %get-tuple-element.41), channel_id=1, source_target_pairs={{0,64},{32,96},{64,0},{96,32},{1,65},{33,97},{65,1},{97,33},{2,66}... | collective-permute-start | bytes 294920 | tf_op jit(solution)/shard_map/ppermute | solution.py:52
  211.9 21.2 %collective-permute-start.9 = (bf16[128,384]{1,0:T(8,128)(2,1)S(1)}, bf16[128,384]{1,0:T(8,128)(2,1)S(1)}, u32[]{:S(2)}, u32[]{:S(2)}) collective-permute-start(bf16[128,384]{1,0:T(8,128)(2,1)S(1)} %get-tuple-element.42), channel_id=1, source_target_pairs={{0,96},{32,0},{64,32},{96,64},{1,97},{33,1},{65,33},{97,65},{2,98}... | collective-permute-start | bytes 294920 | tf_op jit(solution)/shard_map/ppermute | solution.py:52
Sparse Core Ops, SparseCore 0:
  111.5 25.5 all-gather.5
Sparse Core Ops, SparseCore 1:
  170.6 24.6 reduce-scatter.1

commit v5 on v4

--- a/solution.py
+++ b/solution.py
@@ -397,7 +397,8 @@
     gathered = trade(summed, "zl").reshape(256, 1024)
     events_grad = lay_out(spread(gathered, "x"))
     grads = lax.psum_scatter(grads, "y", scatter_dimension=0, tiled=True)
-    pieces = turn(regroup(ids, grads), "zh")
+    pieces = regroup(ids, grads)
+    pieces = [pieces[0]] + [shift(pieces[k], "zh", k) for k in (2, 1, 3)]
     grads = sum(piece.astype(F32) for piece in pieces).astype(BF16)
     return (attended, events_grad, grads[:, :128], grads[:, 128:256], grads[:, 256:])
 

time: 244 us -> 241 us (0.988)
  waiting for transfers between devices: 33.5 us -> 30.2 us
    ppermute x6, waiting for transfers between devices: 14.6 us -> 11.3 us  [shift(): return lax.ppermute(piece, axis, [(i, (i + k) % 4) for i in range(4)])]
where the time goes in v5:
time: 241 us; the launch traced here: 240 us
  blocking collectives  103 us (43%)
  starting transfers between devices  58.9 us (24%)
  waiting for transfers between devices  30.2 us (13%)
  Pallas kernels  22 us (9%)
  between operations  15.8 us (7%)
  local copies, waits for them, and re-layouts  8.79 us (4%)
    ppermute x6, starting transfers between devices, shift(): return lax.ppermute(piece, axis, [(i, (i + k) % 4) for i in range(4)])  28.6 us
    all_gather x1, blocking collectives, on_device(): own = spread(lax.all_gather(shard, 'zh'), 'y').reshape(2048, 384)  27.8 us
    all_to_all x1, blocking collectives, spread(): lax.all_to_all(jnp.broadcast_to(array[None], (count, *array.shape)), axis...  20.2 us
    all_gather x1, blocking collectives, on_device(): near = lax.all_gather(local_state, ('zh', 'core'))  19.5 us
    all_gather x1, blocking collectives, on_device(): near = lax.all_gather(local_grad, ('zh', 'core'))  19.4 us
    all_to_all x3, waiting for transfers between devices, trade(): return lax.all_to_all(pieces, axis, 0, 0)  17.8 us
    all_to_all x1, blocking collectives, trade(): return lax.all_to_all(pieces, axis, 0, 0)  16.2 us
    ppermute x4, starting transfers between devices, swap(): return lax.ppermute(array, 'core', ((0, 1), (1, 0)))  15.1 us
  transfers between devices with their start and end apart: 16, of which 5 were waited for; matrix products, arithmetic and copies ran while one was open for 1% of the time, Pallas kernels for 6%

profile of v5, /device:TPU:1, one launch (start us, length us, event | category | flops | bytes accessed | tf_op | source)
XLA Modules:
  0.0 239.8 jit_solution(10981185228311227554)
XLA Ops:
  8.8 27.8 %all-gather = bf16[512,384]{1,0:T(8,128)(2,1)S(1)} all-gather(bf16[128,384]{1,0:T(8,128)(2,1)S(1)} %pad_maximum_fusion), channel_id=2, replica_groups=mesh['y'=4,'zh'=4,'core'=2,'zl'=4,'x'=4] {'zh'}, dimensions={0}, use_global_device_ids=true | all-gather | bytes 491520 | tf_op jit(solution)/shard_map/all_gather | solution.py:374
  36.8 20.2 %all_to_all.30 = bf16[4,4,128,384]{3,2,1,0:T(8,128)(2,1)S(1)} all-to-all(bf16[4,4,128,384]{3,2,1,0:T(8,128)(2,1)S(1)} %broadcast_in_dim.6), channel_id=1, replica_groups=mesh['y'=4,'zh'=4,'core'=2,'zl'=4,'x'=4] {'y'}, dimensions={0} | all-to-all | bytes 3145728 | tf_op jit(solution)/shard_map/all_to_all | solution.py:40
  57.0 7.3 %collective-permute-start = (bf16[2048,384]{1,0:T(8,128)(2,1)S(1)}, bf16[2048,384]{1,0:T(8,128)(2,1)S(1)}, u32[]{:S(2)}, u32[]{:S(2)}) collective-permute-start(bf16[2048,384]{1,0:T(8,128)(2,1)S(1)} %bitcast.14), channel_id=1, source_target_pairs={{0,16},{16,0},{1,17},{17,1},{2,18},{18,2},{3,19},{19,3},{4,20},{20... | collective-permute-start | bytes 4718600 | tf_op jit(solution)/shard_map/ppermute | solution.py:48
  64.5 1.6 copy-done.1
  66.1 2.9 %shard_map.110 = (bf16[256,2048]{1,0:T(8,128)(2,1)S(1)}, bf16[256,2048]{1,0:T(8,128)(2,1)S(1)}, bf16[2048,256]{1,0:T(8,128)(2,1)S(1)}, bf16[2048,256]{1,0:T(8,128)(2,1)}) custom-call(s32[4]{0:T(128)S(1)} %pad_add_fusion.ids.refs_0_, bf16[256,4096]{1,0:T(8,128)(2,1)S(1)} %copy-done.1), custom_call_target="tpu_custom_call" | custom-call | bytes 6291456 | tf_op jit(solution)/shard_map/pallas_call | solution.py:88
  70.0 1.5 shard_map.111
  72.1 19.5 %all-gather.1 = bf16[1024,128]{1,0:T(8,128)(2,1)S(1)} all-gather(bf16[128,128]{1,0:T(8,128)(2,1)S(1)} %get-tuple-element.29), channel_id=3, replica_groups=mesh['y'=4,'zh'=4,'core'=2,'zl'=4,'x'=4] {'zh','core'}, dimensions={0}, use_global_device_ids=true | all-gather | bytes 294912 | tf_op jit(solution)/shard_map/all_gather | solution.py:378
  92.9 3.3 %all-to-all-start.1 = ((bf16[4,128,128]{2,1,0:T(8,128)(2,1)}), bf16[4,128,128]{2,1,0:T(8,128)(2,1)S(1)}, u32[]{:S(2)}, u32[]{:S(2)}) async-start(bf16[4,128,128]{2,1,0:T(8,128)(2,1)} %shard_map.113), calls=%async_computation.1 | async-start | bytes 262144 | tf_op jit(solution)/shard_map/all_to_all | solution.py:44
  96.3 1.7 shard_map.116
  98.0 3.1 %collective-permute-start.1 = (bf16[512,384]{1,0:T(8,128)(2,1)}, bf16[512,384]{1,0:T(8,128)(2,1)S(1)}, u32[]{:S(2)}, u32[]{:S(2)}) collective-permute-start(bf16[512,384]{1,0:T(8,128)(2,1)} %get-tuple-element.34), channel_id=1, source_target_pairs={{0,1},{1,2},{2,3},{3,0},{4,5},{5,6},{6,7},{7,4},{8,9},{9,10},{10,1... | collective-permute-start | bytes 1179656 | tf_op jit(solution)/shard_map/ppermute | solution.py:52
  101.1 4.4 %collective-permute-start.2 = (bf16[512,384]{1,0:T(8,128)(2,1)}, bf16[512,384]{1,0:T(8,128)(2,1)S(1)}, u32[]{:S(2)}, u32[]{:S(2)}) collective-permute-start(bf16[512,384]{1,0:T(8,128)(2,1)} %get-tuple-element.35), channel_id=1, source_target_pairs={{0,2},{1,3},{2,0},{3,1},{4,6},{5,7},{6,4},{7,5},{8,10},{9,11},{10,... | collective-permute-start | bytes 1179656 | tf_op jit(solution)/shard_map/ppermute | solution.py:52
  105.5 3.1 %collective-permute-start.3 = (bf16[512,384]{1,0:T(8,128)(2,1)S(1)}, bf16[512,384]{1,0:T(8,128)(2,1)S(1)}, u32[]{:S(2)}, u32[]{:S(2)}) collective-permute-start(bf16[512,384]{1,0:T(8,128)(2,1)S(1)} %get-tuple-element.36), channel_id=1, source_target_pairs={{0,3},{1,0},{2,1},{3,2},{4,7},{5,4},{6,5},{7,6},{8,11},{9,8},{10,9... | collective-permute-start | bytes 1179656 | tf_op jit(solution)/shard_map/ppermute | solution.py:52
  109.5 1.9 shard_map.114
  111.4 19.4 %all-gather.3 = bf16[1024,128]{1,0:T(8,128)(2,1)S(1)} all-gather(bf16[128,128]{1,0:T(8,128)(2,1)S(1)} %get-tuple-element.32), channel_id=5, replica_groups=mesh['y'=4,'zh'=4,'core'=2,'zl'=4,'x'=4] {'zh','core'}, dimensions={0}, use_global_device_ids=true | all-gather | bytes 294912 | tf_op jit(solution)/shard_map/all_gather | solution.py:386
  133.1 2.1 collective-permute-start.4
  135.2 2.3 collective-permute-start.5
  137.4 4.6 %all-to-all-start.2 = ((bf16[16,128,128]{2,1,0:T(8,128)(2,1)}), bf16[16,128,128]{2,1,0:T(8,128)(2,1)S(1)}, u32[]{:S(2)}, u32[]{:S(2)}) async-start(bf16[16,128,128]{2,1,0:T(8,128)(2,1)} %bitcast.9.after), calls=%async_computation.2 | async-start | bytes 1048576 | tf_op jit(solution)/shard_map/all_to_all | solution.py:44
  142.0 10.9 %all-to-all-done.2 = bf16[16,128,128]{2,1,0:T(8,128)(2,1)S(1)} async-done(((bf16[16,128,128]{2,1,0:T(8,128)(2,1)}), bf16[16,128,128]{2,1,0:T(8,128)(2,1)S(1)}, u32[]{:S(2)}, u32[]{:S(2)}) %all-to-all-start.2) | async-done | bytes 524320 | tf_op jit(solution)/shard_map/all_to_all | solution.py:44
  155.5 3.5 %shard_map.119 = bf16[256,1024]{1,0:T(8,128)(2,1)S(1)} custom-call(s32[4]{0:T(128)S(1)} %pad_add_fusion.ids.refs_0_, bf16[4,256,640]{2,1,0:T(8,128)(2,1)S(1)} %bitcast.22, bf16[4,4,128,128]{3,2,1,0:T(8,128)(2,1)S(1)} %bitcast.18, bf16[4,512,384]{2,1,0:T(8,128)(2,1)S(1)} %shard_map.117.own, bf16[4,512,384]{2,1,0:T(8,128)(2,1)} %collective-permute-done.4.other, ...), custom_call_target="tpu_custom_call" | custom-call | flops 805306368 | bytes 5242880 | tf_op jit(solution)/shard_map/pallas_call | solution.py:289
  159.8 3.6 %all-to-all-start.3 = ((bf16[4,64,1024]{2,1,0:T(8,128)(2,1)}), bf16[4,64,1024]{2,1,0:T(8,128)(2,1)S(1)}, u32[]{:S(2)}, u32[]{:S(2)}) async-start(bf16[4,64,1024]{2,1,0:T(8,128)(2,1)} %bitcast.21), calls=%async_computation.3 | async-start | bytes 1048576 | tf_op jit(solution)/shard_map/all_to_all | solution.py:44
  163.4 3.5 %collective-permute-start.6 = (bf16[256,384]{1,0:T(8,128)(2,1)S(1)}, bf16[256,384]{1,0:T(8,128)(2,1)S(1)}, u32[]{:S(2)}, u32[]{:S(2)}) collective-permute-start(bf16[256,384]{1,0:T(8,128)(2,1)S(1)} %shard_map.118.after.parts), channel_id=1, source_target_pairs={{0,16},{16,0},{1,17},{17,1},{2,18},{18,2},{3,19},{19,3},{4,20},{20... | collective-permute-start | bytes 589832 | tf_op jit(solution)/shard_map/ppermute | solution.py:48
  168.0 2.5 %shard_map.122 = bf16[2048,384]{1,0:T(8,128)(2,1)} custom-call(bf16[2048,256]{1,0:T(8,128)(2,1)S(1)} %copy-done.4, bf16[2048,256]{1,0:T(8,128)(2,1)S(1)} %collective-permute-done.5.after.crossed, bf16[256,384]{1,0:T(8,128)(2,1)S(1)} %shard_map.118.after.parts, bf16[256,384]{1,0:T(8,128)(2,1)S(1)} %collective-permute-done.6.other), custom_call_target="tpu_custom_call" | custom-call | flops 805306368 | bytes 5242880 | tf_op jit(solution)/shard_map/pallas_call | solution.py:314
  170.5 6.9 %all-to-all-done.3.pieces = bf16[4,64,1024]{2,1,0:T(8,128)(2,1)S(1)} async-done(((bf16[4,64,1024]{2,1,0:T(8,128)(2,1)}), bf16[4,64,1024]{2,1,0:T(8,128)(2,1)S(1)}, u32[]{:S(2)}, u32[]{:S(2)}) %all-to-all-start.3) | async-done | bytes 524320 | tf_op jit(solution)/shard_map/all_to_all | solution.py:44
  177.4 16.2 %all_to_all.31 = bf16[4,64,1024]{2,1,0:T(8,128)(2,1)S(1)} all-to-all(bf16[4,64,1024]{2,1,0:T(8,128)(2,1)S(1)} %shard_map.120), channel_id=1, replica_groups=mesh['y'=4,'zh'=4,'core'=2,'zl'=4,'x'=4] {'zl'}, dimensions={0} | all-to-all | bytes 1048576 | tf_op jit(solution)/shard_map/all_to_all | solution.py:44
  193.6 1.6 broadcast_in_dim.15
  195.3 3.6 %all-to-all-start.5 = ((bf16[4,256,1024]{2,1,0:T(8,128)(2,1)}), bf16[4,256,1024]{2,1,0:T(8,128)(2,1)S(1)}, u32[]{:S(2)}, u32[]{:S(2)}) async-start(bf16[4,256,1024]{2,1,0:T(8,128)(2,1)} %broadcast_in_dim.15), calls=%async_computation.5 | async-start | bytes 4194304 | tf_op jit(solution)/shard_map/all_to_all | solution.py:40
  200.5 8.8 %collective-permute-start.7 = (bf16[128,384]{1,0:T(8,128)(2,1)S(1)}, bf16[128,384]{1,0:T(8,128)(2,1)S(1)}, u32[]{:S(2)}, u32[]{:S(2)}) collective-permute-start(bf16[128,384]{1,0:T(8,128)(2,1)S(1)} %get-tuple-element.40), channel_id=1, source_target_pairs={{0,64},{32,96},{64,0},{96,32},{1,65},{33,97},{65,1},{97,33},{2,66}... | collective-permute-start | bytes 294920 | tf_op jit(solution)/shard_map/ppermute | solution.py:52
  209.3 2.6 %collective-permute-start.8 = (bf16[128,384]{1,0:T(8,128)(2,1)S(1)}, bf16[128,384]{1,0:T(8,128)(2,1)S(1)}, u32[]{:S(2)}, u32[]{:S(2)}) collective-permute-start(bf16[128,384]{1,0:T(8,128)(2,1)S(1)} %get-tuple-element.41), channel_id=1, source_target_pairs={{0,32},{32,64},{64,96},{96,0},{1,33},{33,65},{65,97},{97,1},{2,34}... | collective-permute-start | bytes 294920 | tf_op jit(solution)/shard_map/ppermute | solution.py:52
  211.9 6.6 %collective-permute-start.9 = (bf16[128,384]{1,0:T(8,128)(2,1)S(1)}, bf16[128,384]{1,0:T(8,128)(2,1)S(1)}, u32[]{:S(2)}, u32[]{:S(2)}) collective-permute-start(bf16[128,384]{1,0:T(8,128)(2,1)S(1)} %get-tuple-element.42), channel_id=1, source_target_pairs={{0,96},{32,0},{64,32},{96,64},{1,97},{33,1},{65,33},{97,65},{2,98}... | collective-permute-start | bytes 294920 | tf_op jit(solution)/shard_map/ppermute | solution.py:52
  218.5 4.6 %collective-permute-done.8 = bf16[128,384]{1,0:T(8,128)(2,1)S(1)} collective-permute-done((bf16[128,384]{1,0:T(8,128)(2,1)S(1)}, bf16[128,384]{1,0:T(8,128)(2,1)S(1)}, u32[]{:S(2)}, u32[]{:S(2)}) %collective-permute-start.8) | collective-permute-done | bytes 98336 | tf_op jit(solution)/shard_map/ppermute | solution.py:52
  223.2 6.6 %collective-permute-done.9 = bf16[128,384]{1,0:T(8,128)(2,1)S(1)} collective-permute-done((bf16[128,384]{1,0:T(8,128)(2,1)S(1)}, bf16[128,384]{1,0:T(8,128)(2,1)S(1)}, u32[]{:S(2)}, u32[]{:S(2)}) %collective-permute-start.9) | collective-permute-done | bytes 98336 | tf_op jit(solution)/shard_map/ppermute | solution.py:52
  230.5 1.8 shard_map.121
  (49 shorter events, 14.0 us)
Async XLA Ops:
  57.0 12.9 %collective-permute-start = (bf16[2048,384]{1,0:T(8,128)(2,1)S(1)}, bf16[2048,384]{1,0:T(8,128)(2,1)S(1)}, u32[]{:S(2)}, u32[]{:S(2)}) collective-permute-start(bf16[2048,384]{1,0:T(8,128)(2,1)S(1)} %bitcast.14), channel_id=1, source_target_pairs={{0,16},{16,0},{1,17},{17,1},{2,18},{18,2},{3,19},{19,3},{4,20},{20... | collective-permute-start | bytes 4718600 | tf_op jit(solution)/shard_map/ppermute | solution.py:48
  64.5 1.6 copy-start.1
  69.0 1.0 copy-start.3
  70.0 21.7 %copy-start.8 = (f32[1,128,128]{2,1,0:T(8,128)S(1)}, f32[1,128,128]{2,1,0:T(8,128)}, u32[]{:S(2)}) copy-start(f32[1,128,128]{2,1,0:T(8,128)} %refs_2_.1) | copy-start | bytes 196612
  71.4 0.7 copy-start.6
  72.1 36.4 %copy-start.9 = (s32[2,2]{1,0:T(2,128)S(1)}, s32[2,2]{1,0:T(2,128)}, u32[]{:S(2)}) copy-start(s32[2,2]{1,0:T(2,128)} %mask.3) | copy-start | bytes 52
  72.1 37.3 %copy-start.10 = (bf16[256,128]{1,0:T(8,128)(2,1)S(1)}, bf16[256,128]{1,0:T(8,128)(2,1)}, u32[]{:S(2)}) copy-start(bf16[256,128]{1,0:T(8,128)(2,1)} %cotangent.1) | copy-start | bytes 196612
  72.1 36.4 %copy-start.7 = (bf16[256,384]{1,0:T(8,128)(2,1)S(1)}, bf16[256,384]{1,0:T(8,128)(2,1)}, u32[]{:S(2)}) copy-start(bf16[256,384]{1,0:T(8,128)(2,1)} %copy-done.6) | copy-start | bytes 589828
  92.9 16.5 %all-to-all-start.1 = ((bf16[4,128,128]{2,1,0:T(8,128)(2,1)}), bf16[4,128,128]{2,1,0:T(8,128)(2,1)S(1)}, u32[]{:S(2)}, u32[]{:S(2)}) async-start(bf16[4,128,128]{2,1,0:T(8,128)(2,1)} %shard_map.113), calls=%async_computation.1 | async-start | bytes 262144 | tf_op jit(solution)/shard_map/all_to_all | solution.py:44
  96.3 57.9 %all-gather.6.cloned.1.call-start = ((), (), s32[]{:S(2)}) async-start(), calls=%async_computation.8 | async-start | bytes 1638400 | tf_op jit(solution)/shard_map/all_gather | solution.py:385
  98.0 34.3 %collective-permute-start.1 = (bf16[512,384]{1,0:T(8,128)(2,1)}, bf16[512,384]{1,0:T(8,128)(2,1)S(1)}, u32[]{:S(2)}, u32[]{:S(2)}) collective-permute-start(bf16[512,384]{1,0:T(8,128)(2,1)} %get-tuple-element.34), channel_id=1, source_target_pairs={{0,1},{1,2},{2,3},{3,0},{4,5},{5,6},{6,7},{7,4},{8,9},{9,10},{10,1... | collective-permute-start | bytes 1179656 | tf_op jit(solution)/shard_map/ppermute | solution.py:52
  101.1 31.2 %collective-permute-start.2 = (bf16[512,384]{1,0:T(8,128)(2,1)}, bf16[512,384]{1,0:T(8,128)(2,1)S(1)}, u32[]{:S(2)}, u32[]{:S(2)}) collective-permute-start(bf16[512,384]{1,0:T(8,128)(2,1)} %get-tuple-element.35), channel_id=1, source_target_pairs={{0,2},{1,3},{2,0},{3,1},{4,6},{5,7},{6,4},{7,5},{8,10},{9,11},{10,... | collective-permute-start | bytes 1179656 | tf_op jit(solution)/shard_map/ppermute | solution.py:52
  105.5 26.8 %collective-permute-start.3 = (bf16[512,384]{1,0:T(8,128)(2,1)S(1)}, bf16[512,384]{1,0:T(8,128)(2,1)S(1)}, u32[]{:S(2)}, u32[]{:S(2)}) collective-permute-start(bf16[512,384]{1,0:T(8,128)(2,1)S(1)} %get-tuple-element.36), channel_id=1, source_target_pairs={{0,3},{1,0},{2,1},{3,2},{4,7},{5,4},{6,5},{7,6},{8,11},{9,8},{10,9... | collective-permute-start | bytes 1179656 | tf_op jit(solution)/shard_map/ppermute | solution.py:52
  133.1 21.0 %collective-permute-start.4 = (bf16[4,512,384]{2,1,0:T(8,128)(2,1)S(1)}, bf16[4,512,384]{2,1,0:T(8,128)(2,1)}, u32[]{:S(2)}, u32[]{:S(2)}) collective-permute-start(bf16[4,512,384]{2,1,0:T(8,128)(2,1)S(1)} %shard_map.117.own), channel_id=1, source_target_pairs={{0,16},{16,0},{1,17},{17,1},{2,18},{18,2},{3,19},{19,3},{4,20},{20... | collective-permute-start | bytes 4718600 | tf_op jit(solution)/shard_map/ppermute | solution.py:48
  135.2 6.9 %collective-permute-start.5 = (bf16[2048,256]{1,0:T(8,128)(2,1)}, bf16[2048,256]{1,0:T(8,128)(2,1)S(1)}, u32[]{:S(2)}, u32[]{:S(2)}) collective-permute-start(bf16[2048,256]{1,0:T(8,128)(2,1)} %get-tuple-element.37), channel_id=1, source_target_pairs={{0,16},{16,0},{1,17},{17,1},{2,18},{18,2},{3,19},{19,3},{4,20},{20... | collective-permute-start | bytes 3145736 | tf_op jit(solution)/shard_map/ppermute | solution.py:48
  137.4 15.5 %all-to-all-start.2 = ((bf16[16,128,128]{2,1,0:T(8,128)(2,1)}), bf16[16,128,128]{2,1,0:T(8,128)(2,1)S(1)}, u32[]{:S(2)}, u32[]{:S(2)}) async-start(bf16[16,128,128]{2,1,0:T(8,128)(2,1)} %bitcast.9.after), calls=%async_computation.2 | async-start | bytes 1048576 | tf_op jit(solution)/shard_map/all_to_all | solution.py:44
  154.2 1.3 copy-start.2
  159.0 0.8 copy-start
  159.8 8.2 %copy-start.4 = (bf16[2048,256]{1,0:T(8,128)(2,1)S(1)}, bf16[2048,256]{1,0:T(8,128)(2,1)}, u32[]{:S(2)}) copy-start(bf16[2048,256]{1,0:T(8,128)(2,1)} %copy-done.3) | copy-start | bytes 3145732
  159.8 17.6 %all-to-all-start.3 = ((bf16[4,64,1024]{2,1,0:T(8,128)(2,1)}), bf16[4,64,1024]{2,1,0:T(8,128)(2,1)S(1)}, u32[]{:S(2)}, u32[]{:S(2)}) async-start(bf16[4,64,1024]{2,1,0:T(8,128)(2,1)} %bitcast.21), calls=%async_computation.3 | async-start | bytes 1048576 | tf_op jit(solution)/shard_map/all_to_all | solution.py:44
  163.4 35.5 %reduce-scatter.2.cloned.1.call-start = ((), (), s32[]{:S(2)}) async-start(), calls=%async_computation.7 | async-start | bytes 1966080 | tf_op jit(solution)/shard_map/reduce_scatter | solution.py:399
  163.4 4.5 %collective-permute-start.6 = (bf16[256,384]{1,0:T(8,128)(2,1)S(1)}, bf16[256,384]{1,0:T(8,128)(2,1)S(1)}, u32[]{:S(2)}, u32[]{:S(2)}) collective-permute-start(bf16[256,384]{1,0:T(8,128)(2,1)S(1)} %shard_map.118.after.parts), channel_id=1, source_target_pairs={{0,16},{16,0},{1,17},{17,1},{2,18},{18,2},{3,19},{19,3},{4,20},{20... | collective-permute-start | bytes 589832 | tf_op jit(solution)/shard_map/ppermute | solution.py:48
  195.3 35.3 %all-to-all-start.5 = ((bf16[4,256,1024]{2,1,0:T(8,128)(2,1)}), bf16[4,256,1024]{2,1,0:T(8,128)(2,1)S(1)}, u32[]{:S(2)}, u32[]{:S(2)}) async-start(bf16[4,256,1024]{2,1,0:T(8,128)(2,1)} %broadcast_in_dim.15), calls=%async_computation.5 | async-start | bytes 4194304 | tf_op jit(solution)/shard_map/all_to_all | solution.py:40
  198.9 1.0 copy-start.5
  200.5 18.0 %collective-permute-start.7 = (bf16[128,384]{1,0:T(8,128)(2,1)S(1)}, bf16[128,384]{1,0:T(8,128)(2,1)S(1)}, u32[]{:S(2)}, u32[]{:S(2)}) collective-permute-start(bf16[128,384]{1,0:T(8,128)(2,1)S(1)} %get-tuple-element.40), channel_id=1, source_target_pairs={{0,64},{32,96},{64,0},{96,32},{1,65},{33,97},{65,1},{97,33},{2,66}... | collective-permute-start | bytes 294920 | tf_op jit(solution)/shard_map/ppermute | solution.py:52
  209.3 13.8 %collective-permute-start.8 = (bf16[128,384]{1,0:T(8,128)(2,1)S(1)}, bf16[128,384]{1,0:T(8,128)(2,1)S(1)}, u32[]{:S(2)}, u32[]{:S(2)}) collective-permute-start(bf16[128,384]{1,0:T(8,128)(2,1)S(1)} %get-tuple-element.41), channel_id=1, source_target_pairs={{0,32},{32,64},{64,96},{96,0},{1,33},{33,65},{65,97},{97,1},{2,34}... | collective-permute-start | bytes 294920 | tf_op jit(solution)/shard_map/ppermute | solution.py:52
  211.9 17.9 %collective-permute-start.9 = (bf16[128,384]{1,0:T(8,128)(2,1)S(1)}, bf16[128,384]{1,0:T(8,128)(2,1)S(1)}, u32[]{:S(2)}, u32[]{:S(2)}) collective-permute-start(bf16[128,384]{1,0:T(8,128)(2,1)S(1)} %get-tuple-element.42), channel_id=1, source_target_pairs={{0,96},{32,0},{64,32},{96,64},{1,97},{33,1},{65,33},{97,65},{2,98}... | collective-permute-start | bytes 294920 | tf_op jit(solution)/shard_map/ppermute | solution.py:52
Sparse Core Ops, SparseCore 0:
  111.5 25.5 all-gather.5
Sparse Core Ops, SparseCore 1:
  170.6 24.6 reduce-scatter.1
